TPU v7x, 32 devices: a whole 2x2x4 slice. The times are simulated.
32 devices in a mesh: seq: 8 (over z, x), tensor: 4 (over y, core).
Axes of the slice: x: 2, y: 2, z: 4, core: 2. Of those that a mesh axis runs over, the one named last changes fastest.
Arguments:
- x_in: bfloat16 [8192, 2048], P('seq'), may hold values from -6 to 6
- norm_gain: float32 [2048], replicated, may hold values from 0.5 to 1.5
- w_zx: bfloat16 [2048, 2, 4096], P(None, None, 'tensor'), may hold values from -0.125 to 0.125
- w_bc: bfloat16 [2048, 256], replicated, may hold values from -0.125 to 0.125
- w_dt: bfloat16 [2048, 64], P(None, 'tensor'), may hold values from -0.125 to 0.125
- conv_x: float32 [5, 4096], P(None, 'tensor'), may hold values from -0.6 to 0.6
- conv_bc: float32 [5, 256], replicated, may hold values from -0.6 to 0.6
- head_params: float32 [3, 64], P(None, 'tensor'), may hold values from -8 to 1.5
- gate_gain: float32 [4096], P('tensor'), may hold values from 0.5 to 1.5
- w_out: bfloat16 [4096, 2048], P('tensor'), may hold values from -0.09375 to 0.09375
- lengths: int32 [6], replicated, may hold values from 256 to 4096, as said below
- grad_out: bfloat16 [8192, 2048], P('seq', 'tensor'), may hold values from -6 to 6
Outputs:
- block_out: bfloat16 [8192, 2048], P('seq', 'tensor')
- grad_x: float32 [8192, 2048], P('seq', 'tensor')
- grad_norm_gain: float32 [2048], replicated
- grad_w_zx: float32 [2048, 2, 4096], P('seq', None, 'tensor')
- grad_w_bc: float32 [2048, 256], replicated
- grad_w_dt: float32 [2048, 64], P('seq', 'tensor')
- grad_conv_x: float32 [5, 4096], P(None, 'tensor')
- grad_conv_bc: float32 [5, 256], replicated
- grad_head: float32 [3, 64], P(None, 'tensor')
- grad_gate_gain: float32 [4096], P('tensor')
- grad_w_out: float32 [4096, 2048], P('tensor', 'seq')
Inputs may be any that keep to these rules, and one draw needn't show every extreme that they name: Each sequence holds at most 4096 tokens, and some sequence holds exactly 4096. The lengths sum to 8192.
All inputs are finite; a program needn't handle non-finite values.
Results may differ from a plain program's by a relative error of at most 0.014.
The roundings to bfloat16 on the way count: a program that leaves them out, or rounds other values in their place, can miss the bound.
Values may be sent and summed in bfloat16 or wider, within the bound.
No kernel may reach another device: no remote copies, remote signals or barrier semaphores. Data moves between devices by JAX's collectives and lax.ppermute only.
A program may use at most 192 MiB of HBM per device.

v0:
```python
from functools import partial

import jax
import jax.numpy as jnp
from jax import lax
from jax.sharding import PartitionSpec as P

HEAD_DIM = 64
STATE = 128
WIDTH = 4
SPAN = 256


eps = 1e-05
highest = lax.Precision.HIGHEST


def prefix(value, axis, join, neutral, backward):
    count = lax.axis_size(axis)
    place = lax.axis_index(axis)
    ahead = count - 1 - place if backward else place
    gathered = jax.tree.map(
        lambda a, kind: lax.all_gather(a.astype(kind), axis), value, (jnp.bfloat16, jnp.bfloat16)
    )
    state = jax.tree.map(lambda a, e: jnp.zeros_like(a) + jnp.asarray(e, a.dtype), value, neutral)

    def one(hop, state):
        source = count - 1 - hop if backward else hop
        return join(
            state,
            jax.tree.map(
                lambda a, own: lax.dynamic_index_in_dim(a, source, 0, False).astype(own.dtype),
                gathered,
                value,
            ),
        )

    return lax.fori_loop(0, ahead, one, state)


def passed_along(block, axis, distance):
    devices = range(lax.axis_size(axis))
    route = [(i - distance, i) for i in devices if i - distance in devices]
    return lax.ppermute(block, axis, route)


def segment_ids(lengths, first_pos, row_count):
    starts = jnp.cumsum(lengths) - lengths
    places = first_pos + jnp.arange(row_count, dtype=jnp.int32)
    return jnp.sum((places[:, None] >= starts[None, :]).astype(jnp.int32), axis=1) - 1


def conv_local(seg_ext, extended, weights):
    row_count = extended.shape[0] - (WIDTH - 1)
    own_seg = seg_ext[WIDTH - 1 :]
    summed = jnp.broadcast_to(weights[WIDTH][None, :], (row_count, extended.shape[1]))
    for tap_row in range(WIDTH):
        window = extended[tap_row : tap_row + row_count]
        is_valid = (seg_ext[tap_row : tap_row + row_count] == own_seg).astype(jnp.float32)[:, None]
        summed = summed + weights[tap_row][None, :] * window * is_valid
    return jax.nn.silu(summed)


def step_sizes(dt_raw, head_rows):
    return (jax.nn.softplus(dt_raw + head_rows[0][None, :]), jnp.exp(head_rows[1]))


def decay_logs(step_blocks, decay_rate):
    return jnp.cumsum(-step_blocks * decay_rate[None, None, :], axis=1)


def span_transforms(seg_blocks, prev_seg, x_blocks, b_blocks, step_blocks, decay_rate):
    log_decay = decay_logs(step_blocks, decay_rate)
    last_log = log_decay[:, -1:, :]
    keep_out = (seg_blocks == seg_blocks[:, -1:]).astype(jnp.float32)
    out_weight = jnp.exp(last_log - log_decay) * keep_out[:, :, None] * step_blocks
    local_state = jnp.einsum(
        "cjhp,cjn->chpn", out_weight[:, :, :, None] * x_blocks, b_blocks, precision=highest
    )
    keep_last = (seg_blocks[:, -1] == prev_seg).astype(jnp.float32)
    decays = jnp.exp(last_log[:, 0, :]) * keep_last[:, None]
    return (decays, local_state)


def span_outputs(
    seg_blocks, prev_seg, x_blocks, b_blocks, c_blocks, step_blocks, decay_rate, entering
):
    log_decay = decay_logs(step_blocks, decay_rate)
    positions = jnp.arange(seg_blocks.shape[1], dtype=jnp.int32)
    lower_mask = positions[:, None] >= positions[None, :]
    same_seq = (seg_blocks[:, :, None] == seg_blocks[:, None, :]) & lower_mask[None]
    decay_t = jnp.swapaxes(log_decay, 1, 2)
    gap_log = decay_t[:, :, :, None] - decay_t[:, :, None, :]
    decay_matrix = jnp.where(same_seq[:, None], jnp.exp(jnp.minimum(gap_log, 0.0)), 0.0)
    gram_matrix = jnp.einsum("cin,cjn->cij", c_blocks, b_blocks, precision=highest)
    mixing = decay_matrix * gram_matrix[:, None] * jnp.swapaxes(step_blocks, 1, 2)[:, :, None, :]
    inside = jnp.einsum("chij,cjhp->cihp", mixing, x_blocks, precision=highest)
    keep_in = (seg_blocks == prev_seg[:, None]).astype(jnp.float32)
    in_weight = jnp.exp(log_decay) * keep_in[:, :, None]
    carried = (
        jnp.einsum("cin,chpn->cihp", c_blocks, entering, precision=highest)
        * in_weight[:, :, :, None]
    )
    return inside + carried


def chain_within(decays, local_state, first_state):

    def advance(held_state, element):
        return (element[0][:, None, None] * held_state + element[1], held_state)

    return lax.scan(advance, first_state, (decays, local_state))


def back_within(decays, entering_grad, last_grad):

    def retreat(carried, element):
        return (element[1] + element[0][:, None, None] * carried, carried)

    return lax.scan(retreat, last_grad, (decays, entering_grad), reverse=True)


def combine(earlier, later):
    return (earlier[0] * later[0], later[0][:, None, None] * earlier[1] + later[1])


def device_chain(device_decay, device_state, reverse):
    identity = (jnp.ones_like(device_decay), jnp.zeros_like(device_state))
    result = prefix((device_decay, device_state), "seq", combine, identity, reverse)
    return result[1]


def per_device(
    x_in,
    norm_gain,
    w_zx,
    w_bc,
    w_dt,
    conv_x,
    conv_bc,
    head_params,
    gate_gain,
    w_out,
    lengths,
    grad_out,
):
    tok_rows = x_in.shape[0]
    heads_here = head_params.shape[1]
    inner_here = gate_gain.shape[0]
    inner_all = inner_here * lax.axis_size("tensor")
    model_width = x_in.shape[1]
    slice_width = grad_out.shape[1]
    block_count = tok_rows // SPAN
    halo_rows = WIDTH - 1
    device = lax.axis_index("seq")
    member = lax.axis_index("tensor")
    seg_full = segment_ids(lengths, device * tok_rows - halo_rows, tok_rows + halo_rows)
    seg_blocks = seg_full[halo_rows:].reshape(block_count, SPAN)
    prev_seg = seg_full[halo_rows - 1 : halo_rows - 1 + tok_rows].reshape(block_count, SPAN)[:, 0]
    x_float = x_in.astype(jnp.float32)
    x_scale = lax.rsqrt(jnp.mean(x_float * x_float, axis=1, keepdims=True) + eps)
    unit = x_float * x_scale
    normed = (unit * norm_gain[None, :]).astype(jnp.bfloat16)
    zx_weight = w_zx.reshape(model_width, 2 * inner_here)
    zx_proj = jnp.dot(normed, zx_weight, preferred_element_type=jnp.float32)
    gate_in = zx_proj[:, :inner_here]
    bc_proj = jnp.dot(normed, w_bc, preferred_element_type=jnp.float32)
    dt_raw = jnp.dot(normed, w_dt, preferred_element_type=jnp.float32)
    conv_input = jnp.concatenate([zx_proj[:, inner_here:], bc_proj], axis=1).astype(jnp.bfloat16)
    halo_input = passed_along(conv_input[tok_rows - halo_rows :], "seq", 1)
    extended = jnp.concatenate([halo_input, conv_input], axis=0).astype(jnp.float32)
    conv_weights = jnp.concatenate([conv_x, conv_bc], axis=1)
    conv_out, conv_pull = jax.vjp(partial(conv_local, seg_full), extended, conv_weights)
    acts = lax.optimization_barrier(conv_out.astype(jnp.bfloat16)).astype(jnp.float32)
    x_blocks = acts[:, :inner_here].reshape(block_count, SPAN, heads_here, HEAD_DIM)
    b_blocks = acts[:, inner_here : inner_here + STATE].reshape(block_count, SPAN, STATE)
    c_blocks = acts[:, inner_here + STATE :].reshape(block_count, SPAN, STATE)
    sizes_out, sizes_pull = jax.vjp(step_sizes, dt_raw, head_params[:2])
    step_blocks = sizes_out[0].reshape(block_count, SPAN, heads_here)
    decay_rate = sizes_out[1]
    trans_out, trans_pull = jax.vjp(
        partial(span_transforms, seg_blocks, prev_seg), x_blocks, b_blocks, step_blocks, decay_rate
    )
    decays, local_state = trans_out
    empty_state = jnp.zeros(local_state.shape[1:], jnp.float32)
    device_state, _ = chain_within(decays, local_state, empty_state)
    device_decay = jnp.prod(decays, axis=0)
    arriving = device_chain(device_decay, device_state, False)
    _, entering = chain_within(decays, local_state, arriving)
    inner_out, inner_pull = jax.vjp(
        partial(span_outputs, seg_blocks, prev_seg),
        x_blocks,
        b_blocks,
        c_blocks,
        step_blocks,
        decay_rate,
        entering,
    )
    skip_gain = head_params[2]
    mixed = (inner_out + skip_gain[None, None, :, None] * x_blocks).reshape(tok_rows, inner_here)
    gate_act = jax.nn.silu(gate_in)
    gated = mixed * gate_act
    square_sums = lax.psum(jnp.sum(gated * gated, axis=1), "tensor")
    gate_scale = lax.rsqrt(square_sums / inner_all + eps)[:, None]
    gate_unit = gated * gate_scale
    gate_normed = (gate_unit * gate_gain[None, :]).astype(jnp.bfloat16)
    branch = jnp.dot(gate_normed, w_out, preferred_element_type=jnp.float32)
    branch_part = lax.psum_scatter(
        branch.astype(jnp.bfloat16), "tensor", scatter_dimension=1, tiled=True
    ).astype(jnp.float32)
    x_part = lax.dynamic_slice_in_dim(x_float, member * slice_width, slice_width, 1)
    block_out = (x_part + branch_part).astype(jnp.bfloat16)
    back_dims = (((1,), (1,)), ((), ()))
    weight_dims = (((0,), (0,)), ((), ()))
    cotangent = lax.all_gather(grad_out, "tensor", axis=1, tiled=True)
    grad_gate_normed = lax.dot_general(
        cotangent, w_out, back_dims, preferred_element_type=jnp.float32
    )
    grad_w_out_here = lax.dot_general(
        gate_normed, cotangent, weight_dims, preferred_element_type=jnp.float32
    )
    grad_gate_gain_here = jnp.sum(grad_gate_normed * gate_unit, axis=0)
    grad_unit = grad_gate_normed * gate_gain[None, :]
    row_dots = lax.psum(jnp.sum(grad_unit * gate_unit, axis=1), "tensor")
    grad_gated = gate_scale * (grad_unit - gate_unit * (row_dots / inner_all)[:, None])
    grad_mixed = grad_gated * gate_act
    gate_sig = jax.nn.sigmoid(gate_in)
    grad_gate_in = (grad_gated * mixed * gate_sig * (1.0 + gate_in * (1.0 - gate_sig))).astype(
        jnp.bfloat16
    )
    grad_blocks = grad_mixed.reshape(block_count, SPAN, heads_here, HEAD_DIM)
    grad_skip = jnp.sum(grad_blocks * x_blocks, axis=(0, 1, 3))
    grad_x_inner, grad_b_inner, grad_c_inner, grad_step_inner, grad_rate_inner, grad_entering = (
        inner_pull(grad_blocks)
    )
    device_grad, _ = back_within(decays, grad_entering, empty_state)
    leaving_grad = device_chain(device_decay, device_grad, True)
    _, span_grads = back_within(decays, grad_entering, leaving_grad)
    grad_decays = jnp.sum(span_grads * entering, axis=(2, 3))
    grad_x_trans, grad_b_trans, grad_step_trans, grad_rate_trans = trans_pull(
        (grad_decays, span_grads)
    )
    grad_x_conv = (
        grad_x_inner + grad_x_trans + skip_gain[None, None, :, None] * grad_blocks
    ).reshape(tok_rows, inner_here)
    grad_b_conv = (grad_b_inner + grad_b_trans).reshape(tok_rows, STATE)
    grad_c_conv = grad_c_inner.reshape(tok_rows, STATE)
    grad_steps = (grad_step_inner + grad_step_trans).reshape(tok_rows, heads_here)
    grad_dt_raw, grad_head_rows = sizes_pull((grad_steps, grad_rate_inner + grad_rate_trans))
    grad_extended, grad_conv_w = conv_pull(
        jnp.concatenate([grad_x_conv, grad_b_conv, grad_c_conv], axis=1)
    )
    halo_grad = passed_along(grad_extended[:halo_rows], "seq", -1)
    grad_input = (
        grad_extended[halo_rows:].at[tok_rows - halo_rows :].add(halo_grad).astype(jnp.bfloat16)
    )
    grad_dt_low = grad_dt_raw.astype(jnp.bfloat16)
    grad_zx = jnp.concatenate([grad_gate_in, grad_input[:, :inner_here]], axis=1)
    grad_bc = grad_input[:, inner_here:]
    grad_normed_here = (
        lax.dot_general(grad_zx, zx_weight, back_dims, preferred_element_type=jnp.float32)
        + lax.dot_general(grad_bc, w_bc, back_dims, preferred_element_type=jnp.float32)
        + lax.dot_general(grad_dt_low, w_dt, back_dims, preferred_element_type=jnp.float32)
    )
    grad_zx_here = lax.dot_general(
        normed, grad_zx, weight_dims, preferred_element_type=jnp.float32
    ).reshape(model_width, 2, inner_here)
    grad_bc_here = lax.dot_general(normed, grad_bc, weight_dims, preferred_element_type=jnp.float32)
    grad_dt_here = lax.dot_general(
        normed, grad_dt_low, weight_dims, preferred_element_type=jnp.float32
    )
    unit_part = lax.dynamic_slice_in_dim(unit, member * slice_width, slice_width, 1)
    gain_part = lax.dynamic_slice_in_dim(norm_gain, member * slice_width, slice_width, 0)
    grad_normed = lax.psum(grad_normed_here.astype(jnp.bfloat16), "tensor").astype(jnp.float32)
    row_mean = jnp.mean(grad_normed * norm_gain[None, :] * unit, axis=1, keepdims=True)
    grad_normed_part = lax.dynamic_slice_in_dim(grad_normed, member * slice_width, slice_width, 1)
    grad_unit_part = grad_normed_part * gain_part[None, :]
    grad_x = x_scale * (grad_unit_part - unit_part * row_mean) + grad_out.astype(jnp.float32)
    gain_grad_part = jnp.sum(grad_normed_part * unit_part, axis=0)
    grad_norm_gain_here = lax.dynamic_update_slice_in_dim(
        jnp.zeros((model_width,), jnp.float32), gain_grad_part, member * slice_width, 0
    )
    grad_w_zx, grad_w_dt, grad_w_out = (
        lax.psum_scatter(
            grad_zx_here.astype(jnp.bfloat16), "seq", scatter_dimension=0, tiled=True
        ).astype(jnp.float32),
        lax.psum_scatter(
            grad_dt_here.astype(jnp.bfloat16), "seq", scatter_dimension=0, tiled=True
        ).astype(jnp.float32),
        lax.psum_scatter(
            grad_w_out_here.astype(jnp.bfloat16), "seq", scatter_dimension=1, tiled=True
        ).astype(jnp.float32),
    )
    grad_head_here = jnp.concatenate([grad_head_rows, grad_skip[None, :]], axis=0)
    grad_conv_x, grad_head, grad_gate_gain = lax.psum(
        (grad_conv_w[:, :inner_here], grad_head_here, grad_gate_gain_here), "seq"
    )
    grad_w_bc, grad_conv_bc, grad_norm_gain = lax.psum(
        (grad_bc_here, grad_conv_w[:, inner_here:], grad_norm_gain_here), ("seq", "tensor")
    )
    return (
        block_out,
        grad_x,
        grad_norm_gain,
        grad_w_zx,
        grad_w_bc,
        grad_w_dt,
        grad_conv_x,
        grad_conv_bc,
        grad_head,
        grad_gate_gain,
        grad_w_out,
    )


def solution(mesh):
    return jax.shard_map(
        per_device,
        mesh=mesh,
        in_specs=(
            P("seq", None),
            P(),
            P(None, None, "tensor"),
            P(),
            P(None, "tensor"),
            P(None, "tensor"),
            P(),
            P(None, "tensor"),
            P("tensor"),
            P("tensor", None),
            P(),
            P("seq", "tensor"),
        ),
        out_specs=(
            P("seq", "tensor"),
            P("seq", "tensor"),
            P(),
            P("seq", None, "tensor"),
            P(),
            P("seq", "tensor"),
            P(None, "tensor"),
            P(),
            P(None, "tensor"),
            P("tensor"),
            P("tensor", "seq"),
        ),
        check_vma=False,
    )
```

profile of v0, /device:TPU:0, one launch (start us, length us, event | category | flops | bytes accessed | tf_op | source)
XLA Modules:
  0.0 1095.1 jit_solution(703664194672377306)
XLA Ops:
  10.4 10.3 copy.378
  20.8 11.3 %fusion.98 = f32[1024,2048]{1,0:T(8,128)S(1)} fusion(bf16[2048,2048]{1,0:T(8,128)(2,1)} %bitcast.230, f32[2048]{0:T(1024)S(1)} %copy-done.63, f32[1024]{0:T(1024)S(1)} %add_rsqrt_fusion.1, bf16[1024,2048]{1,0:T(8,128)(2,1)S(1)} %copy-done.6), kind=kOutput, calls=%fused_computation.212 | convolution fusion | flops 8598323200 | bytes 20983808 | tf_op jit(solution)/shard_map/dot_general | solution.py:165
  37.0 5.6 collective-permute-start
  66.2 6.1 multiply_convert_fusion.1
  76.5 7.2 reshape.443
  83.8 7.7 copy.319
  95.9 9.5 while.85
  110.6 19.4 %all-reduce.12 = bf16[128]{0:T(256)(128)(2,1)S(1)} all-reduce(bf16[128]{0:T(256)(128)(2,1)S(1)} %dynamic-update-slice.3), channel_id=2, replica_groups=mesh['seq'=8,'tensor'=4] {'seq'}, use_global_device_ids=true, to_apply=%add.12 | all-reduce | flops 128 | bytes 512
  135.2 6.4 reshape.442
  141.6 5.8 copy.313
  148.6 8.4 all-gather.9.cloned.1.call-done
  158.7 11.0 %while.82 = (s32[]{:T(128)}, f32[16,64,128]{2,1,0:T(8,128)S(1)}, f32[4,16,64,128]{3,2,1,0:T(8,128)}, f32[4,16]{1,0:T(4,128)}, f32[4,16,64,128]{3,2,1,0:T(8,128)}, /*index=5*/s32[]{:T(128)}) while((s32[]{:T(128)}, f32[16,64,128]{2,1,0:T(8,128)S(1)}, f32[4,16,64,128]{3,2,1,0:T(8,128)}, f32[4,16]{1,0:T(4,128)}, f32[4,16,64,128]{3,2,1,0:T(8,128)}, ...), condition=%wide.region_11.12_spmd, body=%wide.region_10.11_spmd.sunk | while | flops 262146 | bytes 2622221 | solution.py:112
  175.4 14.4 %fusion.31 = f32[4,256,16,64]{1,3,2,0:T(8,128)} fusion(f32[4,256,16,64]{1,3,2,0:T(8,128)S(1)} %copy-done.2, f32[4,256,16,64]{1,3,2,0:T(8,128)S(1)} %fusion.111, bf16[4,256,16,64]{1,3,2,0:T(8,128)(2,1)S(1)} %copy-done.25, f32[4,16,256]{2,1,0:T(8,128)S(1)} %copy-done.55, f32[4,256,256]{2,1,0:T(8,128)S(1)} %fusion.110, f32[4,16,256]{2,1,0:T(8,128)S(1)} %copy-done.34, ...), kind=kOutput, calls=%fused_computation.70 | convolution fusion | flops 3246391296 | bytes 16187456 | tf_op jit(solution)/shard_map/jvp(chij,cjhp->cihp)/dot_general | solution.py:97
  189.7 8.1 copy.373
  197.8 7.6 reshape.444
  205.5 6.6 multiply_reduce_fusion.11
  212.0 5.8 psum.63
  217.9 11.9 %multiply_reduce_fusion.6 = (f32[1024]{0:T(1024)}, f32[1024]{0:T(1024)S(1)}, f32[1024,1024]{1,0:T(8,128)}) fusion(f32[1024,1024]{1,0:T(8,128)} %get-tuple-element.510, f32[1024]{0:T(1024)S(1)} %add_rsqrt_fusion, f32[1024]{0:T(1024)S(1)} %copy-done.69, bf16[1024,2048]{1,0:T(8,128)(2,1)} %all-gather.7.cloned.1.call-done, bf16[1024,2048]{1,0:T(8,128)(2,1)} %param.35), kind=kOutput, calls=%fused_computation.71 | convolution fusion | flops 4301256704 | bytes 16793600 | tf_op jit(solution)/shard_map/dot_general | solution.py:216
  229.8 6.7 psum.64
  236.4 10.6 multiply_reduce_fusion.7
  247.1 5.3 copy.326
  252.4 5.6 reshape.409
  262.7 6.8 while.86
  271.7 27.7 %fusion.50 = (f32[4,16,256]{2,1,0:T(8,128)}, f32[4,16,256]{2,1,0:T(8,128)}, f32[4,16,256]{2,1,0:T(8,128)}, f32[4,256,256]{2,1,0:T(8,128)}) fusion(f32[4,16,256]{2,1,0:T(8,128)} %copy-done.33, f32[4,256,256]{2,1,0:T(8,128)} %copy-done.27, f32[4,16,256]{2,1,0:T(8,128)} %copy.312, pred[4,256,256]{2,1,0:T(8,128)(4,1)} %compare_and_fusion, ...), kind=kOutput, calls=%fused_computation.103 | convolution fusion | flops 3300605952 | bytes 8978432 | tf_op jit(solution)/shard_map/transpose(jvp(chij,cjhp->cihp))/dot_general | solution.py:97
  301.6 5.0 multiply_reduce_fusion.9
  310.6 9.9 reduce-window.42
  327.0 8.3 while.83
  336.9 8.2 while.84
  348.6 5.7 multiply_reduce_fusion.8
  357.7 9.9 reduce-window.44
  379.8 10.1 convolution_convert_fusion.2
  391.5 8.9 fusion.63
  402.4 7.5 fusion.60
  409.9 17.5 %fusion.30 = f32[4,256,16,64]{1,3,2,0:T(8,128)} fusion(f32[4,256,16,64]{1,3,2,0:T(8,128)S(1)} %copy-done.24, f32[4,256,16,64]{1,0,3,2:T(4,128)S(1)} %copy-done.5, f32[16]{0:T(128)S(1)} %copy-done.78, f32[4,256,16]{1,2,0:T(8,128)S(1)} %copy-done.29, f32[4,16,256]{2,1,0:T(8,128)} %copy.312, f32[4,256,256]{2,1,0:T(8,128)S(1)} %copy-done.28, ...), kind=kOutput, calls=%fused_computation.68 | convolution fusion | flops 3246391296 | bytes 18284608 | tf_op jit(solution)/shard_map/transpose(jvp(chij,cjhp->cihp))/dot_general | solution.py:97
  427.5 8.1 copy.364
  435.6 8.1 reshape.440
  445.8 14.2 %multiply_reduce_fusion.5 = (f32[1280]{0:T(1024)S(1)}, f32[1280]{0:T(1024)S(1)}, f32[1280]{0:T(1024)S(1)}, f32[1280]{0:T(1024)S(1)}, f32[1280]{0:T(1024)S(1)}, /*index=5*/f32[1024,1280]{1,0:T(8,128)S(1)}) fusion(f32[1027,1280]{1,0:T(8,128)} %copy-done.1, f32[1024]{0:T(1024)S(1)} %copy-done.52, f32[1024]{0:T(1024)S(1)} %copy-done.54, f32[1024]{0:T(1024)S(1)} %copy-done.50, ...), kind=kLoop, calls=%fused_computation.58 | loop fusion | flops 30140160 | bytes 36738048 | tf_op jit(solution)/shard_map/transpose(jvp())/reduce_sum | solution.py:60
  475.8 12.2 %fusion.46 = f32[1024,2048]{1,0:T(8,128)S(1)} fusion(bf16[2048,2048]{1,0:T(8,128)(2,1)} %bitcast.231, bf16[1024,1024]{1,0:T(8,128)(2,1)S(1)} %slice.211, bf16[1024,1024]{1,0:T(8,128)(2,1)} %get-tuple-element.515), kind=kOutput, calls=%fused_computation.98 | convolution fusion | flops 8598323200 | bytes 20971520 | tf_op jit(solution)/shard_map/dot_general | solution.py:261
  492.8 10.2 convolution_convert_fusion.1
  503.7 13.8 %convolution_convert_fusion = bf16[2048,2048]{0,1:T(8,128)(2,1)} fusion(bf16[1024,1024]{1,0:T(8,128)(2,1)S(1)} %slice.211, bf16[1024,1024]{1,0:T(8,128)(2,1)} %get-tuple-element.515, f32[2048]{0:T(1024)S(1)} %copy-done.64, f32[1024]{0:T(1024)S(1)} %copy-done.57, bf16[1024,2048]{1,0:T(8,128)(2,1)} %param.26), kind=kOutput, calls=%fused_computation.50 | convolution fusion | flops 8610906112 | bytes 16789504 | tf_op jit(solution)/shard_map/dot_general | solution.py:265
  517.5 21.5 %copy.357 = bf16[2048,2,1024]{2,1,0:T(2,128)(2,1)} copy(bf16[2048,2,1024]{0,2,1:T(8,128)(2,1)} %bitcast.232) | data formatting | bytes 16777216 | tf_op jit(solution)/shard_map/convert_element_type | solution.py:285
  539.1 6.7 convert_element_type.158
  547.5 37.0 %all-reduce.15 = (f32[5,1024]{1,0:T(8,128)}, f32[3,16]{1,0:T(4,128)}, f32[1024]{0:T(1024)}) all-reduce(f32[5,1024]{1,0:T(8,128)S(1)} %slice.217, f32[3,16]{1,0:T(4,128)S(1)} %pad_maximum_fusion.5, f32[1024]{0:T(1024)S(1)} %copy-done.68), channel_id=1, replica_groups=mesh['seq'=8,'tensor'=4] {'seq'}, use_global_device_ids=true, to_apply=%region_47.48 | all-reduce | flops 6192 | bytes 49536 | tf_op jit(solution)/shard_map/psum | solution.py:295
  584.5 5.2 fusion.75
  603.5 38.4 %all-reduce.14 = (f32[2048]{0:T(1024)}, f32[5,256]{1,0:T(8,128)}) all-reduce(f32[2048]{0:T(1024)S(1)} %dynamic_update_slice.16, f32[5,256]{1,0:T(8,128)S(1)} %pad_add_fusion.4), channel_id=1, replica_groups=mesh['seq'=8,'tensor'=4] {'seq','tensor'}, use_global_device_ids=true, to_apply=%region_38.39 | all-reduce | flops 3328 | bytes 26624 | tf_op jit(solution)/shard_map/psum | solution.py:298
  641.9 29.0 %reduce-scatter.8.cloned.1.call-done = bf16[1024,256]{1,0:T(8,128)(2,1)} async-done(((bf16[1024,2048]{1,0:T(8,128)(2,1)}), bf16[1024,256]{1,0:T(8,128)(2,1)}) %reduce-scatter.8.cloned.1.call-update) | async-done | bytes 524304 | tf_op jit(solution)/shard_map/reduce_scatter | solution.py:290
  672.9 272.5 %all-reduce.24.cloned.1.call-done = bf16[2048,2,1024]{2,1,0:T(2,128)(2,1)} async-done(((bf16[2048,2,1024]{2,1,0:T(2,128)(2,1)}), bf16[2048,2,1024]{2,1,0:T(2,128)(2,1)}) %all-reduce.24.cloned.1.call-update) | async-done | bytes 8388624
  948.7 136.4 %all-reduce.22.cloned.1.call-done = f32[2048,256]{1,0:T(8,128)} async-done(((f32[2048,256]{1,0:T(8,128)}), f32[2048,256]{1,0:T(8,128)}) %all-reduce.22.cloned.1.call-update) | async-done | bytes 2097168 | tf_op jit(solution)/shard_map/psum | solution.py:298
  (377 shorter events, 191.2 us)
Async XLA Ops:
  7.2 25.3 %copy-start = (bf16[2048,256]{1,0:T(8,128)(2,1)S(1)}, bf16[2048,256]{1,0:T(8,128)(2,1)}, u32[]{:S(2)}) copy-start(bf16[2048,256]{1,0:T(8,128)(2,1)} %param.29) | copy-start | bytes 3145732
  7.2 149.8 %all-gather.9.cloned.1.call-start = ((), (), s32[]{:S(2)}) async-start(), calls=%async_computation.9 | async-start | bytes 2359296 | tf_op jit(solution)/shard_map/all_gather | solution.py:23
  10.4 33.6 %copy-start.56 = (f32[1024]{0:T(1024)}, f32[1024]{0:T(1024)S(1)}, u32[]{:S(2)}) copy-start(f32[1024]{0:T(1024)S(1)} %add_rsqrt_fusion.1) | copy-start | bytes 12292
  10.4 10.3 copy-start.6
  10.4 10.3 copy-start.63
  32.5 10.2 copy-start.79
  32.5 11.0 %copy-start.74 = (f32[3,16]{1,0:T(4,128)S(1)}, f32[3,16]{1,0:T(4,128)}, u32[]{:S(2)}) copy-start(f32[3,16]{1,0:T(4,128)} %param.33) | copy-start | bytes 580
  32.5 11.5 %copy-start.47 = (bf16[2048,16]{0,1:T(8,128)(2,1)S(1)}, bf16[2048,16]{0,1:T(8,128)(2,1)}, u32[]{:S(2)}) copy-start(bf16[2048,16]{0,1:T(8,128)(2,1)} %param.30) | copy-start | bytes 196612
  37.0 27.6 %collective-permute-start = (bf16[3,1280]{1,0:T(4,128)(2,1)}, bf16[3,1280]{1,0:T(4,128)(2,1)}, u32[]{:S(2)}, u32[]{:S(2)}) collective-permute-start(bf16[3,1280]{1,0:T(4,128)(2,1)} %pad_maximum_fusion.4), channel_id=1, source_target_pairs={{0,4},{4,8},{8,12},{12,16},{16,20},{20,24},{24,28},{1,5},{5,9},{9,... | collective-permute-start | bytes 23048 | tf_op jit(solution)/shard_map/ppermute | solution.py:44
  43.1 23.1 %copy-start.49 = (f32[1024]{0:T(1024)}, f32[1024]{0:T(1024)S(1)}, u32[]{:S(2)}) copy-start(f32[1024]{0:T(1024)S(1)} %get-tuple-element.533) | copy-start | bytes 12292
  43.1 23.1 %copy-start.51 = (f32[1024]{0:T(1024)}, f32[1024]{0:T(1024)S(1)}, u32[]{:S(2)}) copy-start(f32[1024]{0:T(1024)S(1)} %get-tuple-element.534) | copy-start | bytes 12292
  43.1 23.1 %copy-start.53 = (f32[1024]{0:T(1024)}, f32[1024]{0:T(1024)S(1)}, u32[]{:S(2)}) copy-start(f32[1024]{0:T(1024)S(1)} %get-tuple-element.535) | copy-start | bytes 12292
  43.5 14.8 %copy-start.67 = (f32[4]{0:T(128)}, f32[4]{0:T(128)S(1)}, u32[]{:S(2)}) copy-start(f32[4]{0:T(128)S(1)} %convert_reduce_fusion.1) | copy-start | bytes 52
  44.0 16.0 %copy-start.65 = (f32[5,256]{1,0:T(8,128)S(1)}, f32[5,256]{1,0:T(8,128)}, u32[]{:S(2)}) copy-start(f32[5,256]{1,0:T(8,128)} %param.32) | copy-start | bytes 15364
  48.1 16.4 %copy-start.14 = (bf16[1024,1024]{1,0:T(8,128)(2,1)S(1)}, bf16[1024,1024]{1,0:T(8,128)(2,1)}, u32[]{:S(2)}) copy-start(bf16[1024,1024]{1,0:T(8,128)(2,1)} %copy-done.13) | copy-start | bytes 6291460
  48.2 17.9 %copy-start.32 = (f32[4,256,16]{1,0,2:T(4,128)}, f32[4,256,16]{1,0,2:T(4,128)S(1)}, u32[]{:S(2)}) copy-start(f32[4,256,16]{1,0,2:T(4,128)S(1)} %reshape.401) | copy-start | bytes 196612
  95.9 13.2 %copy-start.73 = (u32[32]{0:T(128)S(1)}, u32[32]{0:T(128)}, u32[]{:S(2)}) copy-start(u32[32]{0:T(128)} %constant.263) | copy-start | bytes 388
  95.9 14.4 %copy-start.76 = (bf16[16]{0:T(256)(128)(2,1)S(1)}, bf16[16]{0:T(256)(128)(2,1)}, u32[]{:S(2)}) copy-start(bf16[16]{0:T(256)(128)(2,1)} %get-tuple-element.511) | copy-start | bytes 100
  105.4 36.2 %copy-start.10 = (f32[4,16,64,128]{3,2,1,0:T(8,128)}, f32[4,16,64,128]{3,2,1,0:T(8,128)S(1)}, u32[]{:S(2)}) copy-start(f32[4,16,64,128]{3,2,1,0:T(8,128)S(1)} %get-tuple-element.879) | copy-start | bytes 6291460
  107.6 110.2 %all-gather.7.cloned.1.call-start = ((), (), s32[]{:S(2)}) async-start(), calls=%async_computation.4 | async-start | bytes 5242880 | tf_op jit(solution)/shard_map/all_gather | solution.py:215
  108.3 218.6 %all-gather.11.cloned.1.call-start = ((), (), s32[]{:S(2)}) async-start(), calls=%async_computation.10 | async-start | bytes 2359296 | tf_op jit(solution)/shard_map/all_gather | solution.py:23
  148.6 24.6 %copy-start.27 = (f32[4,256,256]{2,1,0:T(8,128)}, f32[4,256,256]{2,1,0:T(8,128)S(1)}, u32[]{:S(2)}) copy-start(f32[4,256,256]{2,1,0:T(8,128)S(1)} %fusion.110) | copy-start | bytes 3145732
  158.7 16.7 %copy-start.36 = (pred[4,256,256]{2,1,0:T(8,128)(4,1)S(1)}, pred[4,256,256]{2,1,0:T(8,128)(4,1)}, u32[]{:S(2)}) copy-start(pred[4,256,256]{2,1,0:T(8,128)(4,1)} %compare_and_fusion) | copy-start | bytes 786436
  205.5 12.4 %copy-start.69 = (f32[1024]{0:T(1024)S(1)}, f32[1024]{0:T(1024)}, u32[]{:S(2)}) copy-start(f32[1024]{0:T(1024)} %param.34) | copy-start | bytes 12292
  269.5 29.9 %copy-start.11 = (f32[4,16,64,128]{3,2,1,0:T(8,128)}, f32[4,16,64,128]{3,2,1,0:T(8,128)S(1)}, u32[]{:S(2)}) copy-start(f32[4,16,64,128]{3,2,1,0:T(8,128)S(1)} %get-tuple-element.880) | copy-start | bytes 6291460
  271.6 318.1 %reduce-scatter.6.cloned.1.call-start = ((), (), s32[]{:S(2)}) async-start(), calls=%async_computation.7 | async-start | bytes 73728 | tf_op jit(solution)/shard_map/reduce_scatter | solution.py:287
  336.9 10.9 copy-start.20
  354.9 20.7 %copy-start.57 = (f32[1024]{0:T(1024)S(1)}, f32[1024]{0:T(1024)}, u32[]{:S(2)}) copy-start(f32[1024]{0:T(1024)} %copy-done.56) | copy-start | bytes 12292
  379.7 211.4 %reduce-scatter.4.cloned.1.call-start = ((), (), s32[]{:S(2)}) async-start(), calls=%async_computation.3 | async-start | bytes 5242880 | tf_op jit(solution)/shard_map/reduce_scatter | solution.py:208
  389.9 12.5 %copy-start.29 = (f32[4,256,16]{1,2,0:T(8,128)S(1)}, f32[4,256,16]{1,2,0:T(8,128)}, u32[]{:S(2)}) copy-start(f32[4,256,16]{1,2,0:T(8,128)} %copy.317) | copy-start | bytes 196612
  389.9 204.4 %all-reduce.20.cloned.1.call-start = ((), (), s32[]{:S(2)}) async-start(), calls=%async_computation.5 | async-start | bytes 8388608 | tf_op jit(solution)/shard_map/psum | solution.py:274
  391.5 10.9 copy-start.4
  391.5 10.9 copy-start.9
  391.5 18.5 %copy-start.28 = (f32[4,256,256]{2,1,0:T(8,128)S(1)}, f32[4,256,256]{2,1,0:T(8,128)}, u32[]{:S(2)}) copy-start(f32[4,256,256]{2,1,0:T(8,128)} %copy-done.27) | copy-start | bytes 3145732
  400.3 9.6 copy-start.5
  435.5 10.2 copy-start.50
  435.5 10.2 copy-start.52
  435.5 10.2 copy-start.54
  445.8 14.3 %copy-start.40 = (f32[1280]{0:T(1024)S(1)}, f32[1280]{0:T(1024)}, u32[]{:S(2)}) copy-start(f32[1280]{0:T(1024)} %copy-done.39) | copy-start | bytes 15364
  445.8 14.3 %copy-start.42 = (f32[1280]{0:T(1024)S(1)}, f32[1280]{0:T(1024)}, u32[]{:S(2)}) copy-start(f32[1280]{0:T(1024)} %copy-done.41) | copy-start | bytes 15364
  445.8 14.3 %copy-start.44 = (f32[1280]{0:T(1024)S(1)}, f32[1280]{0:T(1024)}, u32[]{:S(2)}) copy-start(f32[1280]{0:T(1024)} %copy-done.43) | copy-start | bytes 15364
  445.8 14.3 %copy-start.46 = (f32[1280]{0:T(1024)S(1)}, f32[1280]{0:T(1024)}, u32[]{:S(2)}) copy-start(f32[1280]{0:T(1024)} %copy-done.45) | copy-start | bytes 15364
  462.0 10.5 collective-permute-start.1
  473.9 14.1 %slice-start = ((s8[8388608]{0:T(1024)(128)(4,1)}), s8[4194304]{0:T(1024)(128)(4,1)S(1)}, s32[]{:S(2)}) async-start(s8[8388608]{0:T(1024)(128)(4,1)} %bitcast.224), calls=%async_computation.12 | async-start | bytes 8388608
  475.8 12.2 %slice-start.1 = ((s8[8388608]{0:T(1024)(128)(4,1)}), s8[4194304]{0:T(1024)(128)(4,1)S(1)}, s32[]{:S(2)}) async-start(s8[8388608]{0:T(1024)(128)(4,1)} %bitcast.224), calls=%async_computation.13 | async-start | bytes 8388608
  492.5 178.3 %reduce-scatter.8.cloned.1.call-start = ((), (), s32[]{:S(2)}) async-start(), calls=%async_computation.8 | async-start | bytes 4718592 | tf_op jit(solution)/shard_map/reduce_scatter | solution.py:290
  503.0 442.4 %all-reduce.24.cloned.1.call-start = ((), (), s32[]{:S(2)}) async-start(), calls=%async_computation.11 | async-start | bytes 16777216
  539.0 546.0 %all-reduce.22.cloned.1.call-start = ((), (), s32[]{:S(2)}) async-start(), calls=%async_computation.6 | async-start | bytes 4194304 | tf_op jit(solution)/shard_map/psum | solution.py:298
  (45 other events, 220.2 us)
Sparse Core Ops, SparseCore 0:
  107.7 49.2 all-gather.8
  158.6 32.9 all-gather.6
  271.8 55.1 all-gather.10
  379.8 50.9 reduce-scatter.5
  433.2 43.5 reduce-scatter.3
  492.6 84.9 all-reduce.19
  581.2 89.5 reduce-scatter.7
  675.2 270.1 all-reduce.23
  952.2 132.8 all-reduce.21
where the time goes:
time: 1110 us; the launch traced here: 1100 us
  waiting for transfers between devices  450 us (41%)
  matrix products  193 us (17%)
  local copies, waits for them, and re-layouts  160 us (14%)
  other arithmetic  160 us (14%)
  blocking collectives  107 us (10%)
  between operations  16.9 us (2%)
    unnamed x10, waiting for transfers between devices  273 us
    psum x1, waiting for transfers between devices, per_device(): lax.psum((grad_bc_here, grad_conv_w[:, inner_here:], grad_norm_gain_here)...  136 us
    dot_general x3, matrix products, span_outputs(): inside = jnp.einsum('chij,cjhp->cihp', mixing, x_blocks, precision=highest)  59.6 us
    psum x1, blocking collectives, per_device(): lax.psum((grad_bc_here, grad_conv_w[:, inner_here:], grad_norm_gain_here)...  38.4 us
    psum x1, blocking collectives, per_device(): lax.psum((grad_conv_w[:, :inner_here], grad_head_here, grad_gate_gain_her...  37 us
    reduce_scatter x1, waiting for transfers between devices, per_device(): lax.psum_scatter(grad_w_out_here.astype(jnp.bfloat16), 'seq', scatter_dim...  29 us
    reshape x4, local copies, waits for them, and re-layouts, per_device(): acts[:, :inner_here].reshape(block_count, SPAN, heads_here, HEAD_DIM)  27.1 us
    unnamed x171, local copies, waits for them, and re-layouts  24.1 us
  transfers between devices with their start and end apart: 11, of which 5 were waited for; matrix products, arithmetic and copies ran while one was open for 30% of the time, Pallas kernels for 0%

commit v1 on v0

v1 whole, which is shorter than its diff:
```python
from functools import partial

import jax
import jax.numpy as jnp
from jax import lax
from jax.experimental import pallas as pl
from jax.experimental.pallas import tpu as pltpu
from jax.sharding import PartitionSpec as P

HEAD_DIM = 64
STATE = 128
WIDTH = 4
CHUNK = 128
REACH = 4096
PAD = 8
HALO = 16

eps = 1e-05
f32 = jnp.float32
bf16 = jnp.bfloat16
highest = lax.Precision.HIGHEST
vmem_limit = 56 * 1024 * 1024


def nn(a, b):
    return lax.dot_general(a, b, (((1,), (0,)), ((), ())), preferred_element_type=f32)


def nt(a, b):
    return lax.dot_general(a, b, (((1,), (1,)), ((), ())), preferred_element_type=f32)


def exact(a, b):
    return lax.dot_general(
        a, b, (((1,), (0,)), ((), ())), precision=highest, preferred_element_type=f32
    )


def head_map(heads):
    row = lax.broadcasted_iota(jnp.int32, (heads, heads * HEAD_DIM), 0)
    col = lax.broadcasted_iota(jnp.int32, (heads, heads * HEAD_DIM), 1)
    return jnp.where((col >> 6) == row, 1.0, 0.0).astype(bf16)


def spread(v, member):
    high = v.astype(bf16)
    rest = (v - high.astype(f32)).astype(bf16)
    return nn(high, member) + nn(rest, member)


def spread_row(v, member):
    return spread(jnp.broadcast_to(v, (PAD, v.shape[1])), member)[0:1]


def per_head(v, member):
    return nt(v.astype(bf16), member)


def triangle(strict, upper):
    row = lax.broadcasted_iota(jnp.int32, (CHUNK, CHUNK), 0)
    col = lax.broadcasted_iota(jnp.int32, (CHUNK, CHUNK), 1)
    if upper:
        row, col = col, row
    keep = (row > col) if strict else (row >= col)
    return jnp.where(keep, 1.0, 0.0).astype(f32)


def softplus(v):
    return jnp.maximum(v, 0.0) + jnp.log1p(jnp.exp(-jnp.abs(v)))


def sigmoid(v):
    return 1.0 / (1.0 + jnp.exp(-v))


def seg_bounds(info_ref, chunk):
    info = info_ref[...] - chunk * CHUNK
    return info[:, 0:1], info[:, 1:2]


def row_ids():
    return lax.broadcasted_iota(jnp.int32, (CHUNK, 1), 0)


def flag(v):
    return jnp.where(v, 1.0, 0.0).astype(f32)


def conv_pre(ext_ref, w_ref, masks, base, lo, wide):
    cols = slice(base + lo, base + lo + wide)
    taps = slice(lo, lo + wide)
    total = w_ref[WIDTH : WIDTH + 1, taps] + w_ref[WIDTH - 1 : WIDTH, taps] * ext_ref[
        PAD : PAD + CHUNK, cols
    ]
    for back in range(1, WIDTH):
        total = total + w_ref[WIDTH - 1 - back : WIDTH - back, taps] * (
            ext_ref[PAD - back : PAD - back + CHUNK, cols] * masks[back]
        )
    return total


def fwd_kernel(
    ux_ref, ubc_ref, hx_ref, hbc_ref, cx_ref, cbc_ref, dtr_ref, hp_ref, info_ref,
    xa_ref, bca_ref, dt_ref, log_ref, sloc_ref, send_ref,
    ext, held, drun,
):
    chunk = pl.program_id(0)
    inner = ux_ref.shape[1]
    heads = dtr_ref.shape[1]

    @pl.when(chunk == 0)
    def _():
        ext[0:PAD, 0:inner] = hx_ref[...].astype(f32)[HALO - PAD : HALO]
        ext[0:PAD, inner:] = hbc_ref[...].astype(f32)[HALO - PAD : HALO]
        held[...] = jnp.zeros_like(held)
        drun[...] = jnp.ones_like(drun)

    @pl.when(chunk > 0)
    def _():
        ext[0:PAD, :] = ext[CHUNK : CHUNK + PAD, :]

    ext[PAD:, 0:inner] = ux_ref[...].astype(f32)
    ext[PAD:, inner:] = ubc_ref[...].astype(f32)
    first, last = seg_bounds(info_ref, chunk)
    rows = row_ids()
    wide = 256
    masks = [None] + [
        jnp.broadcast_to(flag(rows - back >= first), (CHUNK, wide)) for back in range(1, WIDTH)
    ]
    for lo in range(0, inner, wide):
        pre = conv_pre(ext, cx_ref, masks, 0, lo, wide)
        xa_ref[:, lo : lo + wide] = (pre * sigmoid(pre)).astype(bf16)
    pre = conv_pre(ext, cbc_ref, masks, inner, 0, 2 * STATE)
    bca_ref[...] = (pre * sigmoid(pre)).astype(bf16)

    member = head_map(heads)
    dt = softplus(dtr_ref[...] + hp_ref[0:1, :])
    rate = jnp.exp(hp_ref[1:2, :])
    logs = exact(triangle(False, False), -dt * rate)
    dt_ref[...] = dt
    log_ref[...] = logs
    tail = logs[CHUNK - 1 : CHUNK, :]
    keep_in = flag(first < 0)
    keep_out = flag(last >= CHUNK)
    weight = jnp.exp(tail - logs) * keep_out * dt
    decay = jnp.exp(tail) * keep_in[CHUNK - 1 : CHUNK, :]
    x_in = (xa_ref[...].astype(f32) * spread(weight, member)).astype(bf16)
    b_cols = jnp.transpose(bca_ref[:, 0:STATE].astype(f32)).astype(bf16)
    local = nn(b_cols, x_in)
    decay_all = spread_row(decay, member)
    sloc_ref[...] = held[...].astype(bf16)[None]
    held[...] = decay_all * held[...] + local
    drun[...] = drun[...] * decay_all

    @pl.when(chunk == pl.num_programs(0) - 1)
    def _():
        total = drun[...]
        high = total.astype(bf16)
        send_ref[0:STATE, :] = held[...].astype(bf16)
        send_ref[STATE:, :] = jnp.concatenate(
            [total, total - high.astype(f32)], axis=0
        ).astype(bf16)


def intra_kernel(xa_ref, bca_ref, dt_ref, log_ref, sloc_ref, hp_ref, info_ref, y_ref):
    chunk = pl.program_id(0)
    heads = dt_ref.shape[1]
    member = head_map(heads)
    first, _ = seg_bounds(info_ref, chunk)
    rows = lax.broadcasted_iota(jnp.int32, (CHUNK, CHUNK), 0)
    cols = lax.broadcasted_iota(jnp.int32, (CHUNK, CHUNK), 1)
    b = bca_ref[:, 0:STATE]
    c = bca_ref[:, STATE:]
    mixed = jnp.where((cols <= rows) & (cols >= first), nt(c, b), 0.0)
    logs = log_ref[...]
    keep_in = flag(first < 0)
    logs_t = jnp.transpose(logs)
    x = xa_ref[...].astype(f32)
    xd = x * spread(dt_ref[...], member)
    skip = spread_row(hp_ref[2:3, :], member)
    carried = spread(jnp.exp(logs) * keep_in, member) * nn(c, sloc_ref[0]) + skip * x
    lane = lax.broadcasted_iota(jnp.int32, (1, 2 * HEAD_DIM), 1)
    left = flag(lane < HEAD_DIM)
    right = 1.0 - left
    for pair in range(heads // 2):
        mats = []
        for h in (2 * pair, 2 * pair + 1):
            gap = logs[:, h : h + 1] - logs_t[h : h + 1, :]
            mats.append((jnp.exp(jnp.minimum(gap, 0.0)) * mixed).astype(bf16))
        at = slice(2 * pair * HEAD_DIM, 2 * (pair + 1) * HEAD_DIM)
        xp = xd[:, at]
        block = jnp.concatenate([(xp * left).astype(bf16), (xp * right).astype(bf16)], axis=0)
        y_ref[:, at] = carried[:, at] + nn(jnp.concatenate(mats, axis=1), block)


def gate_sums_kernel(
    yl_ref, bca_ref, log_ref, sloc_ref, sin_ref, z_ref, gg_ref, gain_ref, info_ref,
    y_ref, sent_ref, sums_ref,
    dpre,
):
    chunk = pl.program_id(0)
    heads = log_ref.shape[1]
    member = head_map(heads)

    @pl.when(chunk == 0)
    def _():
        dpre[...] = jnp.ones_like(dpre)

    first, _ = seg_bounds(info_ref, chunk)
    keep_in = flag(first < 0)
    before = dpre[0:1, :]
    gate = jnp.exp(log_ref[...]) * keep_in
    state = sin_ref[...]
    sent_ref[...] = (sloc_ref[0].astype(f32) + spread_row(before, member) * state).astype(bf16)[None]
    carried = spread(gate * before, member) * nn(bca_ref[:, STATE:], state.astype(bf16))
    y = yl_ref[...] + carried
    y_ref[...] = y
    z = z_ref[...]
    gated = y * z * sigmoid(z)
    squares = jnp.sum(gated * gated, axis=1, keepdims=True)
    dots = jnp.sum(gated * gg_ref[...] * gain_ref[...], axis=1, keepdims=True)
    lane = lax.broadcasted_iota(jnp.int32, (CHUNK, STATE), 1)
    both = jnp.where(lane == 0, squares, jnp.where(lane == 1, dots, 0.0))
    sums_ref[...] = jnp.transpose(both)[0:PAD][None]
    dpre[...] = dpre[...] * gate[CHUNK - 1 : CHUNK, :]


def gate_back_kernel(
    y_ref, z_ref, gg_ref, sums_ref, gain_ref, xa_ref, bca_ref, log_ref, info_ref,
    gn_ref, gz_ref, gy_ref, lloc_ref, send_ref, ggain_ref, gskip_ref,
    held, *, inner_all,
):
    step = pl.program_id(0)
    chunk = pl.num_programs(0) - 1 - step
    heads = log_ref.shape[1]
    member = head_map(heads)

    @pl.when(step == 0)
    def _():
        held[...] = jnp.zeros_like(held)
        ggain_ref[...] = jnp.zeros_like(ggain_ref)
        gskip_ref[...] = jnp.zeros_like(gskip_ref)

    sums = jnp.transpose(jnp.concatenate([sums_ref[0]] * (CHUNK // PAD), axis=0))
    scale = lax.rsqrt(sums[:, 0:1] * (1.0 / inner_all) + eps)
    mean = sums[:, 1:2] * scale * (1.0 / inner_all)
    z = z_ref[...]
    y = y_ref[...]
    s = sigmoid(z)
    act = z * s
    gain = gain_ref[...]
    gg = gg_ref[...]
    unit = y * act * scale
    gn_ref[...] = (unit * gain).astype(bf16)
    ggain_ref[...] += jnp.sum(gg * unit, axis=0, keepdims=True)
    g_gated = scale * (gg * gain - unit * mean)
    gz_ref[...] = (g_gated * y * s * (1.0 + z * (1.0 - s))).astype(bf16)
    gy = g_gated * act
    gy_ref[...] = gy.astype(bf16)
    gskip_ref[...] += jnp.sum(gy * xa_ref[...].astype(f32), axis=0, keepdims=True)
    first, _ = seg_bounds(info_ref, chunk)
    into = jnp.exp(log_ref[...]) * flag(first < 0)
    weighted = (gy * spread(into, member)).astype(bf16)
    c_cols = jnp.transpose(bca_ref[:, STATE:].astype(f32)).astype(bf16)
    lloc_ref[...] = held[...].astype(bf16)[None]
    held[...] = spread_row(into[CHUNK - 1 : CHUNK, :], member) * held[...] + nn(c_cols, weighted)

    @pl.when(step == pl.num_programs(0) - 1)
    def _():
        send_ref[...] = held[...].astype(bf16)


def bwd_kernel(
    gy_ref, xa_ref, bca_ref, dt_ref, log_ref, dtr_ref, sent_ref, lloc_ref, lin_ref,
    ux_ref, ubc_ref, px_ref, pbc_ref, hx_ref, hbc_ref, cx_ref, cbc_ref, hp_ref, info_ref,
    gux_ref, gubc_ref, gdt_ref, tailx_ref, tailbc_ref, hgx_ref, hgbc_ref,
    gcx_ref, gcbc_ref, ghead_ref,
    ext, gext, dsuf, rows_scr, head_ext,
):
    step = pl.program_id(0)
    chunk = pl.num_programs(0) - 1 - step
    inner = gy_ref.shape[1]
    heads = log_ref.shape[1]
    member = head_map(heads)
    total_cols = inner + 2 * STATE

    @pl.when(step == 0)
    def _():
        dsuf[...] = jnp.ones_like(dsuf)
        gcx_ref[...] = jnp.zeros_like(gcx_ref)
        gcbc_ref[...] = jnp.zeros_like(gcbc_ref)
        ghead_ref[...] = jnp.zeros_like(ghead_ref)
        gext[CHUNK:, :] = jnp.zeros((PAD, total_cols), f32)

    @pl.when(step > 0)
    def _():
        gext[CHUNK:, :] = gext[0:PAD, :]

    first, last = seg_bounds(info_ref, chunk)
    logs = log_ref[...]
    logs_t = jnp.transpose(logs)
    dt = dt_ref[...]
    tail = logs[CHUNK - 1 : CHUNK, :]
    into = jnp.exp(logs) * flag(first < 0)
    out = jnp.exp(tail - logs) * flag(last >= CHUNK)
    decay = into[CHUNK - 1 : CHUNK, :]
    rate = jnp.exp(hp_ref[1:2, :])

    b = bca_ref[:, 0:STATE]
    c = bca_ref[:, STATE:]
    rows = lax.broadcasted_iota(jnp.int32, (CHUNK, CHUNK), 0)
    cols = lax.broadcasted_iota(jnp.int32, (CHUNK, CHUNK), 1)
    keep = (cols >= rows) & (cols < last)
    mixed = jnp.where(keep, nt(b, c), 0.0)

    lam = lloc_ref[0].astype(f32) + spread_row(dsuf[0:1, :], member) * lin_ref[...]
    lam_low = lam.astype(bf16)
    dsuf[...] = dsuf[...] * decay
    state = sent_ref[0]
    decay_sum = jnp.sum(lam * state.astype(f32), axis=0, keepdims=True) * spread_row(decay, member)
    z_head = per_head(jnp.broadcast_to(decay_sum, (PAD, inner)), member)[0:1]

    x = xa_ref[...].astype(f32)
    gy_low = gy_ref[...]
    gy = gy_low.astype(f32)
    dt_all = spread(dt, member)
    xd = x * dt_all
    out_all = spread(out, member)
    g_out = out_all * nn(b, lam_low)
    into_all = spread(into, member)
    e_head = per_head(xd * g_out, member)
    gy_in = gy * into_all
    f_head = per_head(gy_in * nn(c, state), member)
    g_c = nt(gy_in.astype(bf16), state)
    g_b = nt((xd * out_all).astype(bf16), lam_low)
    skip = spread_row(hp_ref[2:3, :], member)

    lane = lax.broadcasted_iota(jnp.int32, (1, 2 * HEAD_DIM), 1)
    left = flag(lane < HEAD_DIM).astype(bf16)
    right = flag(lane >= HEAD_DIM).astype(bf16)
    side = lax.broadcasted_iota(jnp.int32, (2 * CHUNK, CHUNK), 0) >> 7
    place = lax.broadcasted_iota(jnp.int32, (2 * CHUNK, CHUNK), 1)
    ones = jnp.ones((PAD, CHUNK), bf16)
    mixed2 = jnp.concatenate([mixed, mixed], axis=1)
    d_mixed = jnp.zeros((CHUNK, CHUNK), f32)
    k_sum = jnp.zeros((CHUNK, CHUNK), f32)
    t_head = jnp.zeros((CHUNK, heads), f32)
    for pair in range(heads // 2):
        at = slice(2 * pair * HEAD_DIM, 2 * (pair + 1) * HEAD_DIM)
        gyp = gy_low[:, at]
        block = jnp.concatenate([gyp * left, gyp * right], axis=0)
        d_m = nt(xd[:, at].astype(bf16), block)
        gaps = [logs_t[h : h + 1, :] - logs[:, h : h + 1] for h in (2 * pair, 2 * pair + 1)]
        decays = jnp.exp(jnp.minimum(jnp.concatenate(gaps, axis=1), 0.0))
        w = d_m * decays
        d_mixed = d_mixed + w[:, 0:CHUNK] + w[:, CHUNK:]
        g = (w * mixed2).astype(bf16)
        g_in = nn((decays * mixed2).astype(bf16), block)
        select = jnp.where(place == 2 * pair + side, 1.0, 0.0).astype(bf16)
        k_sum = k_sum + nn(g, select)
        r_pair = nn(ones, g)
        rows_scr[2 * pair : 2 * pair + 1, :] = r_pair[0:1, 0:CHUNK]
        rows_scr[2 * pair + 1 : 2 * pair + 2, :] = r_pair[0:1, CHUNK:]
        g_xd = g_in + g_out[:, at]
        gext[0:CHUNK, at] = dt_all[:, at] * g_xd + skip[:, at] * gy[:, at]
        t_head = t_head + per_head(x[:, at] * g_xd, member[:, at])
    d_mixed = jnp.where(keep, d_mixed, 0.0)
    g_b = g_b + nn(d_mixed.astype(bf16), c)
    g_c = g_c + nn(jnp.transpose(d_mixed).astype(bf16), b)
    gext[0:CHUNK, inner : inner + STATE] = g_b
    gext[0:CHUNK, inner + STATE :] = g_c

    r_head = jnp.transpose(rows_scr[...])[:, 0:heads]
    g_log = r_head - k_sum[:, 0:heads] + f_head
    g_a = exact(triangle(False, True), g_log) + exact(triangle(True, False), e_head) + z_head
    g_dt = (t_head - rate * g_a) * sigmoid(dtr_ref[...] + hp_ref[0:1, :])
    gdt_ref[...] = g_dt.astype(bf16)
    ghead_ref[0:1, :] += jnp.sum(g_dt, axis=0, keepdims=True)
    ghead_ref[1:2, :] += -rate * jnp.sum(dt * g_a, axis=0, keepdims=True)

    start = chunk == 0
    ext[0:PAD, 0:inner] = jnp.where(start, hx_ref[...].astype(f32), px_ref[...].astype(f32))[
        HALO - PAD : HALO
    ]
    ext[0:PAD, inner:] = jnp.where(start, hbc_ref[...].astype(f32), pbc_ref[...].astype(f32))[
        HALO - PAD : HALO
    ]
    ext[PAD:, 0:inner] = ux_ref[...].astype(f32)
    ext[PAD:, inner:] = ubc_ref[...].astype(f32)
    wide = 256
    ids = row_ids()
    masks = [None] + [
        jnp.broadcast_to(flag(ids - back >= first), (CHUNK, wide)) for back in range(1, WIDTH)
    ]
    ahead = [None] + [
        jnp.broadcast_to(flag(ids + back < last), (CHUNK, wide)) for back in range(1, WIDTH)
    ]
    for lo in range(0, total_cols, wide):
        on_x = lo < inner
        w_ref, base = (cx_ref, 0) if on_x else (cbc_ref, inner)
        gc_ref, gu_ref = (gcx_ref, gux_ref) if on_x else (gcbc_ref, gubc_ref)
        tail_ref, hg_ref = (tailx_ref, hgx_ref) if on_x else (tailbc_ref, hgbc_ref)
        here = slice(lo, lo + wide)
        taps = slice(lo - base, lo - base + wide)
        pre = conv_pre(ext, w_ref, masks, base, lo - base, wide)
        s = sigmoid(pre)
        g_pre = gext[0:CHUNK, here] * s * (1.0 + pre * (1.0 - s))
        gext[0:CHUNK, here] = g_pre
        gc_ref[WIDTH : WIDTH + 1, taps] += jnp.sum(g_pre, axis=0, keepdims=True)
        gc_ref[WIDTH - 1 : WIDTH, taps] += jnp.sum(
            g_pre * ext[PAD : PAD + CHUNK, here], axis=0, keepdims=True
        )
        g_u = w_ref[WIDTH - 1 : WIDTH, taps] * g_pre
        for back in range(1, WIDTH):
            tap = WIDTH - 1 - back
            masked = g_pre * masks[back]
            gc_ref[tap : tap + 1, taps] += jnp.sum(
                masked * ext[PAD - back : PAD - back + CHUNK, here], axis=0, keepdims=True
            )
            g_u = g_u + w_ref[tap : tap + 1, taps] * (
                gext[back : back + CHUNK, here] * ahead[back]
            )
        gu_ref[:, taps] = g_u.astype(bf16)

        @pl.when(step == 0)
        def _(g_u=g_u, tail_ref=tail_ref, taps=taps):
            tail_ref[:, taps] = g_u[CHUNK - HALO :, :]

        @pl.when(start)
        def _(g_pre=g_pre, hg_ref=hg_ref, taps=taps, w_ref=w_ref):
            halo = jnp.zeros((PAD, wide), f32)
            head_ext[0:PAD, :] = jnp.zeros((PAD, wide), f32)
            for back in range(1, WIDTH):
                tap = WIDTH - 1 - back
                head_ext[PAD:, :] = g_pre[0:PAD, :] * masks[back][0:PAD, :]
                halo = halo + w_ref[tap : tap + 1, taps] * head_ext[back : back + PAD, :]
            hg_ref[0:PAD, taps] = jnp.zeros((PAD, wide), f32)
            hg_ref[PAD:, taps] = halo


def along(value, axis, distance):
    count = lax.axis_size(axis)
    route = [(i, i + distance) for i in range(count) if 0 <= i + distance < count]
    return lax.ppermute(value, axis, route)


def swapped(value, axis, bit):
    return lax.ppermute(value, axis, [(i, i ^ bit) for i in range(lax.axis_size(axis))])


def all_sum(value, axis):
    bit = 1
    while bit < lax.axis_size(axis):
        value = value + swapped(value, axis, bit)
        bit *= 2
    return value


def gather_columns(value, axis):
    count = lax.axis_size(axis)
    me = lax.axis_index(axis)
    wide = value.shape[1]
    whole = jnp.zeros((value.shape[0], count * wide), value.dtype)
    bit = count // 2
    held = [(0, value)]
    while bit:
        held = held + [(mask ^ bit, swapped(part, axis, bit)) for mask, part in held]
        bit //= 2
    for mask, part in held:
        whole = lax.dynamic_update_slice_in_dim(whole, part, (me ^ mask) * wide, 1)
    return whole


def scatter_columns(value, axis):
    count = lax.axis_size(axis)
    me = lax.axis_index(axis)
    wide = value.shape[1] // count
    parts = {
        mask: lax.dynamic_slice_in_dim(value, (me ^ mask) * wide, wide, 1) for mask in range(count)
    }
    bit = 1
    while bit < count:
        kept = {}
        for mask in parts:
            if not mask & bit:
                other = swapped(parts[mask | bit].astype(bf16), axis, bit)
                kept[mask] = parts[mask].astype(f32) + other.astype(f32)
        parts = kept
        bit *= 2
    return parts[0]


def ring_order(count):
    return list(range(0, count, 2)) + list(range(count - 1, 0, -2))


def ring_scatter(value, axis):
    count = lax.axis_size(axis)
    rows = value.shape[0] // count
    half = value.shape[1] // 2
    order = ring_order(count)
    spot = [order.index(i) for i in range(count)]
    me = lax.axis_index(axis)
    my_spot = jnp.asarray(spot, jnp.int32)[me]
    table = jnp.asarray(order, jnp.int32)
    outs = []
    for sign, cols in ((1, slice(0, half)), (-1, slice(half, value.shape[1]))):
        route = [(order[i], order[(i + sign) % count]) for i in range(count)]
        moving = None
        for hop in range(count):
            owner = table[(my_spot + sign * (count - 1 - hop) + 2 * count) % count]
            mine = lax.dynamic_slice_in_dim(value[:, cols], owner * rows, rows, 0)
            if moving is None:
                moving = mine
            else:
                moving = moving.astype(f32) + mine.astype(f32)
                if hop < count - 1:
                    moving = moving.astype(bf16)
            if hop < count - 1:
                moving = lax.ppermute(moving, axis, route)
        outs.append(moving)
    return jnp.concatenate(outs, axis=1)


def window_chain(sent, decay, axis, sign, reach):
    arrived = [along(sent, axis, sign * hop) for hop in range(1, reach + 1)]
    fades = [along(decay, axis, sign * hop) for hop in range(1, reach)]
    total = arrived[-1].astype(f32)
    for hop in range(reach - 2, -1, -1):
        total = arrived[hop].astype(f32) + fades[hop] * total
    return total


def call(kernel, grid, in_specs, out_specs, out_shape, scratch, flops, moved, **names):
    return pl.pallas_call(
        kernel,
        grid=grid,
        in_specs=in_specs,
        out_specs=out_specs,
        out_shape=out_shape,
        scratch_shapes=scratch,
        compiler_params=pltpu.CompilerParams(
            dimension_semantics=("arbitrary",), vmem_limit_bytes=vmem_limit
        ),
        cost_estimate=pl.CostEstimate(flops=flops, bytes_accessed=moved, transcendentals=0),
        **names,
    )


def per_device(
    x_in, norm_gain, w_zx, w_bc, w_dt, conv_x, conv_bc, head_params, gate_gain, w_out, lengths,
    grad_out,
):
    tokens, width = x_in.shape
    heads = head_params.shape[1]
    inner = gate_gain.shape[0]
    members = lax.axis_size("tensor")
    inner_all = inner * members
    chunks = tokens // CHUNK
    reach = min(-(-REACH // tokens), lax.axis_size("seq") - 1)
    device = lax.axis_index("seq")
    member = lax.axis_index("tensor")

    shape = jax.ShapeDtypeStruct
    rows = lambda wide: pl.BlockSpec((CHUNK, wide), lambda i: (i, 0))
    back = lambda wide: pl.BlockSpec((CHUNK, wide), lambda i: (chunks - 1 - i, 0))
    whole = lambda *dims: pl.BlockSpec(dims, lambda i: (0,) * len(dims))
    stack = lambda *dims: pl.BlockSpec((1,) + dims, lambda i: (i,) + (0,) * len(dims))
    stack_back = lambda *dims: pl.BlockSpec(
        (1,) + dims, lambda i: (chunks - 1 - i,) + (0,) * len(dims)
    )

    ends = jnp.cumsum(lengths)
    starts = ends - lengths
    places = device * tokens + jnp.arange(tokens, dtype=jnp.int32)[:, None]
    seg_first = jnp.max(jnp.where(starts[None, :] <= places, starts[None, :], 0), axis=1)
    seg_last = jnp.min(
        jnp.where(ends[None, :] > places, ends[None, :], jnp.iinfo(jnp.int32).max // 2), axis=1
    )
    info = jnp.stack([seg_first, seg_last], axis=1) - device * tokens

    cotangent = gather_columns(grad_out, "tensor")

    x_float = x_in.astype(f32)
    x_scale = lax.rsqrt(jnp.mean(x_float * x_float, axis=1, keepdims=True) + eps)
    unit = x_float * x_scale
    normed = (unit * norm_gain[None, :]).astype(bf16)
    w_z, w_x = w_zx[:, 0, :], w_zx[:, 1, :]
    u_x = jnp.dot(normed, w_x, preferred_element_type=f32).astype(bf16)
    u_bc = jnp.dot(normed, w_bc, preferred_element_type=f32).astype(bf16)
    dt_raw = jnp.dot(normed, w_dt, preferred_element_type=f32)
    halo_x = along(u_x[tokens - HALO :], "seq", 1)
    halo_bc = along(u_bc[tokens - HALO :], "seq", 1)
    gate_in = jnp.dot(normed, w_z, preferred_element_type=f32)

    acts_x, acts_bc, dt, logs, local_in, leaving = call(
        fwd_kernel, (chunks,),
        [rows(inner), rows(2 * STATE), whole(HALO, inner), whole(HALO, 2 * STATE),
         whole(WIDTH + 1, inner), whole(WIDTH + 1, 2 * STATE), rows(heads), whole(3, heads), rows(2)],
        [rows(inner), rows(2 * STATE), rows(heads), rows(heads), stack(STATE, inner),
         whole(STATE + 2 * PAD, inner)],
        [shape((tokens, inner), bf16), shape((tokens, 2 * STATE), bf16), shape((tokens, heads), f32),
         shape((tokens, heads), f32), shape((chunks, STATE, inner), bf16),
         shape((STATE + 2 * PAD, inner), bf16)],
        [pltpu.VMEM((CHUNK + PAD, inner + 2 * STATE), f32), pltpu.VMEM((STATE, inner), f32),
         pltpu.VMEM((PAD, inner), f32)],
        2 * tokens * inner * STATE, 8 * tokens * inner, name="conv_states",
    )(u_x, u_bc, halo_x, halo_bc, conv_x, conv_bc, dt_raw, head_params, info)

    fade = leaving[STATE:]
    arrived = [along(leaving, "seq", hop) for hop in range(1, reach + 1)]
    state_in = arrived[-1][:STATE].astype(f32)
    for hop in range(reach - 2, -1, -1):
        block = arrived[hop].astype(f32)
        state_in = block[:STATE] + (block[STATE : STATE + 1] + block[STATE + PAD : STATE + PAD + 1]) * state_in

    back_dims = (((1,), (1,)), ((), ()))
    weight_dims = (((0,), (0,)), ((), ()))
    grad_gate = lax.dot_general(cotangent, w_out, back_dims, preferred_element_type=f32)

    y_local = call(
        intra_kernel, (chunks,),
        [rows(inner), rows(2 * STATE), rows(heads), rows(heads), stack(STATE, inner),
         whole(3, heads), rows(2)],
        rows(inner), shape((tokens, inner), f32), [],
        4 * tokens * inner * STATE, 8 * tokens * inner, name="intra",
    )(acts_x, acts_bc, dt, logs, local_in, head_params, info)

    gain_row = gate_gain[None, :]
    mixed, entering, sums = call(
        gate_sums_kernel, (chunks,),
        [rows(inner), rows(2 * STATE), rows(heads), stack(STATE, inner), whole(STATE, inner),
         rows(inner), rows(inner), whole(1, inner), rows(2)],
        [rows(inner), stack(STATE, inner), stack(PAD, CHUNK)],
        [shape((tokens, inner), f32), shape((chunks, STATE, inner), bf16),
         shape((chunks, PAD, CHUNK), f32)],
        [pltpu.VMEM((PAD, heads), f32)],
        2 * tokens * inner * STATE, 20 * tokens * inner, name="gate_sums",
    )(y_local, acts_bc, logs, local_in, state_in, gate_in, grad_gate, gain_row, info)

    sums = all_sum(sums, "tensor")

    gate_normed, grad_gate_in, grad_mixed, grad_local, grad_leaving, grad_gain, grad_skip = call(
        partial(gate_back_kernel, inner_all=inner_all), (chunks,),
        [back(inner), back(inner), back(inner), stack_back(PAD, CHUNK), whole(1, inner),
         back(inner), back(2 * STATE), back(heads), back(2)],
        [back(inner), back(inner), back(inner), stack_back(STATE, inner), whole(STATE, inner),
         whole(1, inner), whole(1, inner)],
        [shape((tokens, inner), bf16), shape((tokens, inner), bf16), shape((tokens, inner), bf16),
         shape((chunks, STATE, inner), bf16), shape((STATE, inner), bf16), shape((1, inner), f32),
         shape((1, inner), f32)],
        [pltpu.VMEM((STATE, inner), f32)],
        2 * tokens * inner * STATE, 20 * tokens * inner, name="gate_back",
    )(mixed, gate_in, grad_gate, sums, gain_row, acts_x, acts_bc, logs, info)

    from_later = [along(grad_leaving, "seq", -hop) for hop in range(1, reach + 1)]
    fades = [along(fade, "seq", -hop) for hop in range(1, reach)]
    grad_in = from_later[-1].astype(f32)
    for hop in range(reach - 2, -1, -1):
        low = fades[hop].astype(f32)
        grad_in = from_later[hop].astype(f32) + (low[0:1] + low[PAD : PAD + 1]) * grad_in

    grad_w_out_t = lax.dot_general(
        cotangent, gate_normed, weight_dims, preferred_element_type=f32
    ).astype(bf16)
    grad_w_out_sum = lax.psum_scatter(grad_w_out_t, "seq", scatter_dimension=0, tiled=True)
    grad_z_here = lax.dot_general(
        normed, grad_gate_in, weight_dims, preferred_element_type=f32
    ).astype(bf16)
    grad_z_sum = ring_scatter(grad_z_here, "seq")
    branch = jnp.dot(gate_normed, w_out, preferred_element_type=f32).astype(bf16)
    branch_part = scatter_columns(branch, "tensor")
    slice_width = grad_out.shape[1]
    x_part = lax.dynamic_slice_in_dim(x_in, member * slice_width, slice_width, 1).astype(f32)
    block_out = (x_part + branch_part).astype(bf16)

    halo_before = lambda wide: pl.BlockSpec(
        (HALO, wide),
        lambda i: (jnp.maximum((chunks - 1 - i) * (CHUNK // HALO) - 1, 0), 0),
    )
    total_cols = inner + 2 * STATE
    (grad_ux, grad_ubc, grad_dt, tail_x, tail_bc, sent_x, sent_bc, grad_cx, grad_cbc, grad_heads) = call(
        bwd_kernel, (chunks,),
        [back(inner), back(inner), back(2 * STATE), back(heads), back(heads), back(heads),
         stack_back(STATE, inner), stack_back(STATE, inner), whole(STATE, inner),
         back(inner), back(2 * STATE), halo_before(inner), halo_before(2 * STATE),
         whole(HALO, inner), whole(HALO, 2 * STATE), whole(WIDTH + 1, inner),
         whole(WIDTH + 1, 2 * STATE), whole(3, heads), back(2)],
        [back(inner), back(2 * STATE), back(heads), whole(HALO, inner), whole(HALO, 2 * STATE),
         whole(HALO, inner), whole(HALO, 2 * STATE), whole(PAD, inner), whole(PAD, 2 * STATE),
         whole(PAD, heads)],
        [shape((tokens, inner), bf16), shape((tokens, 2 * STATE), bf16), shape((tokens, heads), bf16),
         shape((HALO, inner), f32), shape((HALO, 2 * STATE), f32), shape((HALO, inner), f32),
         shape((HALO, 2 * STATE), f32), shape((PAD, inner), f32), shape((PAD, 2 * STATE), f32),
         shape((PAD, heads), f32)],
        [pltpu.VMEM((CHUNK + PAD, total_cols), f32), pltpu.VMEM((CHUNK + PAD, total_cols), f32),
         pltpu.VMEM((PAD, heads), f32), pltpu.VMEM((CHUNK, CHUNK), f32),
         pltpu.VMEM((2 * PAD, 256), f32)],
        12 * tokens * inner * STATE, 20 * tokens * inner, name="scan_back",
    )(grad_mixed, acts_x, acts_bc, dt, logs, dt_raw, entering, grad_local, grad_in,
      u_x, u_bc, u_x, u_bc, halo_x, halo_bc, conv_x, conv_bc, head_params, info)

    tail_x = (tail_x + along(sent_x, "seq", -1)).astype(bf16)
    tail_bc = (tail_bc + along(sent_bc, "seq", -1)).astype(bf16)
    grad_ux = lax.dynamic_update_slice_in_dim(grad_ux, tail_x, tokens - HALO, 0)
    grad_ubc = lax.dynamic_update_slice_in_dim(grad_ubc, tail_bc, tokens - HALO, 0)

    spare = 128 - heads
    grad_bcdt = jnp.concatenate([grad_ubc, grad_dt, jnp.zeros((tokens, spare), bf16)], axis=1)
    grad_x_here = lax.dot_general(normed, grad_ux, weight_dims, preferred_element_type=f32).astype(bf16)
    grad_bcdt_here = lax.dot_general(
        normed, grad_bcdt, weight_dims, preferred_element_type=f32
    ).astype(bf16)
    grad_bcdt_sum = ring_scatter(
        jnp.concatenate([grad_bcdt_here, jnp.zeros((width, 128), bf16)], axis=1), "seq"
    )
    grad_x_sum = ring_scatter(grad_x_here, "seq")

    grad_normed_here = (
        lax.dot_general(grad_gate_in, w_z, back_dims, preferred_element_type=f32)
        + lax.dot_general(grad_ux, w_x, back_dims, preferred_element_type=f32)
        + lax.dot_general(grad_ubc, w_bc, back_dims, preferred_element_type=f32)
        + lax.dot_general(grad_dt, w_dt, back_dims, preferred_element_type=f32)
    )
    row_dots = all_sum(
        jnp.sum(grad_normed_here * unit * norm_gain[None, :], axis=1).reshape(tokens // 128, 128),
        "tensor",
    )
    gain_here = jnp.sum(grad_normed_here * unit, axis=0)
    grad_normed = scatter_columns(grad_normed_here.astype(bf16), "tensor")
    gain_part = lax.dynamic_slice_in_dim(norm_gain, member * slice_width, slice_width, 0)
    row_mean = row_dots.reshape(tokens, 1) * (1.0 / width)
    grad_x = x_scale * (grad_normed * gain_part[None, :] - x_part * x_scale * row_mean) + grad_out.astype(f32)

    shared = jnp.concatenate([grad_cbc[: WIDTH + 1].reshape(-1), gain_here]).reshape(-1, 128)
    shared = all_sum(shared, "tensor")
    heads_here = jnp.concatenate(
        [grad_heads[:2], jnp.sum(grad_skip.reshape(heads, HEAD_DIM), axis=1)[None, :]], axis=0
    )
    own = jnp.concatenate(
        [grad_cx[: WIDTH + 1].reshape(-1), grad_gain.reshape(-1), heads_here.reshape(-1),
         jnp.zeros((-3 * heads % 128,), f32)]
    ).reshape(-1, 128)
    small = all_sum(jnp.concatenate([shared, own], axis=0), "seq")
    shared, own = small[: shared.shape[0]].reshape(-1), small[shared.shape[0] :].reshape(-1)
    bc_size = (WIDTH + 1) * 2 * STATE
    x_size = (WIDTH + 1) * inner
    grad_conv_bc = shared[:bc_size].reshape(WIDTH + 1, 2 * STATE)
    grad_norm_gain = shared[bc_size:]
    grad_conv_x = own[:x_size].reshape(WIDTH + 1, inner)
    grad_gate_gain = own[x_size : x_size + inner]
    grad_head = own[x_size + inner : x_size + inner + 3 * heads].reshape(3, heads)

    bc_rows = all_sum_low(grad_bcdt_sum[:, : 2 * STATE], "tensor").astype(bf16)
    grad_w_bc = lax.all_gather(bc_rows, "seq", axis=0, tiled=True).astype(f32)
    grad_w_dt = grad_bcdt_sum[:, 2 * STATE : 2 * STATE + heads]
    grad_w_zx = jnp.stack([grad_z_sum, grad_x_sum], axis=1)
    grad_w_out = grad_w_out_sum.astype(f32).T
    return (
        block_out, grad_x, grad_norm_gain, grad_w_zx, grad_w_bc, grad_w_dt, grad_conv_x,
        grad_conv_bc, grad_head, grad_gate_gain, grad_w_out,
    )


def all_sum_low(value, axis):
    bit = 1
    while bit < lax.axis_size(axis):
        value = value + swapped(value.astype(bf16), axis, bit).astype(f32)
        bit *= 2
    return value


def solution(mesh):
    return jax.shard_map(
        per_device,
        mesh=mesh,
        in_specs=(
            P("seq", None), P(), P(None, None, "tensor"), P(), P(None, "tensor"),
            P(None, "tensor"), P(), P(None, "tensor"), P("tensor"), P("tensor", None), P(),
            P("seq", "tensor"),
        ),
        out_specs=(
            P("seq", "tensor"), P("seq", "tensor"), P(), P("seq", None, "tensor"), P(),
            P("seq", "tensor"), P(None, "tensor"), P(), P(None, "tensor"), P("tensor"),
            P("tensor", "seq"),
        ),
        check_vma=False,
    )
```

time: 1110 us -> 609 us (0.55)
  waiting for transfers between devices: 450 us -> 139 us
  starting transfers between devices: 8.06 us -> 129 us
  other arithmetic: 160 us -> 44.9 us
  blocking collectives: 107 us -> 0 us
  local copies, waits for them, and re-layouts: 160 us -> 60.2 us
  matrix products: 193 us -> 100 us
  Pallas kernels: 0 us -> 90.2 us
  between operations: 16.9 us -> 35.1 us
    unnamed x10 -> x2, waiting for transfers between devices: 273 us -> 0.03 us
    ppermute x2 -> x77, waiting for transfers between devices: 0.01 us -> 139 us  [the longest x42 88.1 us: ring_scatter(): moving = lax.ppermute(moving, axis, route)]
    psum x2 -> x0, waiting for transfers between devices: 136 us -> none  [the longest x1 136 us: per_device(): lax.psum((grad_bc_here, grad_conv_w[:, inner_here:], grad_norm_gain_here)...]
    ppermute x2 -> x77, starting transfers between devices: 7.03 us -> 129 us  [the longest x42 83.4 us: ring_scatter(): moving = lax.ppermute(moving, axis, route)]
    dot_general x24 -> x14, matrix products: 193 us -> 100 us  [the longest x1 10.4 us: per_device(): lax.dot_general(grad_ux, w_x, back_dims, preferred_element_type=f32)]
    pallas_call x0 -> x5, Pallas kernels: none -> 90.2 us  [the longest x1 42.1 us: per_device(): call(bwd_kernel, (chunks,), [back(inner), back(inner), back(2 * STATE), b...]
    psum x4 -> x0, blocking collectives: 87.8 us -> none  [the longest x1 38.4 us: per_device(): lax.psum((grad_bc_here, grad_conv_w[:, inner_here:], grad_norm_gain_here)...]
    reshape x16 -> x6, local copies, waits for them, and re-layouts: 65.7 us -> 2.71 us  [the longest x1 1.35 us: per_device(): grad_conv_x = own[:x_size].reshape(WIDTH + 1, inner)]
  transfers between devices with their start and end apart: 11 -> 79, of which waited for: 5 -> 36; matrix products, arithmetic and copies ran while one was open for 30% -> 31% of each run, Pallas kernels for 0% -> 8%
where the time goes in v1:
time: 609 us; the launch traced here: 599 us
  waiting for transfers between devices  139 us (23%)
  starting transfers between devices  129 us (21%)
  matrix products  100 us (16%)
  Pallas kernels  90.2 us (15%)
  local copies, waits for them, and re-layouts  60.2 us (10%)
  other arithmetic  44.9 us (7%)
  between operations  35.1 us (6%)
    ppermute x42, waiting for transfers between devices, ring_scatter(): moving = lax.ppermute(moving, axis, route)  88.1 us
    ppermute x42, starting transfers between devices, ring_scatter(): moving = lax.ppermute(moving, axis, route)  83.4 us
    pallas_call x1, Pallas kernels, per_device(): call(bwd_kernel, (chunks,), [back(inner), back(inner), back(2 * STATE), b...  42.1 us
    ppermute x15, starting transfers between devices, along(): return lax.ppermute(value, axis, route)  30.3 us
    ppermute x15, waiting for transfers between devices, along(): return lax.ppermute(value, axis, route)  29.3 us
    ppermute x20, waiting for transfers between devices, swapped(): lax.ppermute(value, axis, [(i, i ^ bit) for i in range(lax.axis_size(axis...  21.6 us
    convert_element_type x36, other arithmetic, ring_scatter(): moving = moving.astype(bf16)  17.5 us
    ppermute x20, starting transfers between devices, swapped(): lax.ppermute(value, axis, [(i, i ^ bit) for i in range(lax.axis_size(axis...  14.9 us
  transfers between devices with their start and end apart: 79, of which 36 were waited for; matrix products, arithmetic and copies ran while one was open for 31% of the time, Pallas kernels for 8%

profile of v1, /device:TPU:0, one launch (start us, length us, event | category | flops | bytes accessed | tf_op | source)
XLA Modules:
  0.0 598.5 jit_solution(14796035628389484319)
XLA Ops:
  10.3 3.2 fusion.3
  15.7 3.4 collective-permute-start.1
  19.1 13.1 %fusion.35 = (bf16[2048,1,1024]{2,1,0:T(2,128)(2,1)}, bf16[2048,1,1024]{2,1,0:T(2,128)(2,1)}) fusion(bf16[2048,2,1024]{2,1,0:T(2,128)(2,1)S(1)} %bitcast.94), kind=kLoop, calls=%fused_computation.134 | loop fusion | bytes 16777216 | tf_op jit(solution)/shard_map/slice | solution.py:588
  32.2 8.9 %convolution_convert_fusion.5.ux_ref.px_ref = bf16[1024,1024]{1,0:T(8,128)(2,1)S(1)} fusion(bf16[2048,1,1024]{2,1,0:T(2,128)(2,1)} %get-tuple-element.113, bf16[1024,2048]{1,0:T(8,128)(2,1)S(1)} %copy-done.1, f32[2048]{0:T(1024)S(1)} %copy-done.27, f32[1024]{0:T(1024)S(1)} %add_rsqrt_fusion), kind=kOutput, calls=%fused_computation.27 | convolution fusion | flops 4304404480 | bytes 10498048 | tf_op jit(solution)/shard_map/dot_general | solution.py:589
  41.2 3.5 collective-permute-start
  46.0 4.4 fusion.31.dtr_ref
  52.4 12.9 %conv_states.1 = (bf16[1024,1024]{1,0:T(8,128)(2,1)}, bf16[1024,256]{1,0:T(8,128)(2,1)}, f32[1024,16]{1,0:T(8,128)}, f32[1024,16]{1,0:T(8,128)}, bf16[8,128,1024...) custom-call(bf16[1024,1024]{1,0:T(8,128)(2,1)} %copy-done.4, bf16[1024,256]{1,0:T(8,128)(2,1)} %copy-done.13, ...), custom_call_target="tpu_custom_call" | custom-call | flops 268435456 | bytes 8388608 | tf_op jit(solution)/shard_map/conv_states/pallas_call | solution.py:596
  65.3 4.4 collective-permute-start.4
  69.8 10.3 %fusion.12.z_ref = f32[1024,1024]{1,0:T(8,128)} fusion(bf16[2048,1,1024]{2,1,0:T(2,128)(2,1)} %get-tuple-element.112, bf16[1024,2048]{1,0:T(8,128)(2,1)S(1)} %copy-done.2, f32[2048]{0:T(1024)S(1)} %copy-done.27, f32[1024]{0:T(1024)S(1)} %add_rsqrt_fusion), kind=kOutput, calls=%fused_computation.30 | convolution fusion | flops 4303355904 | bytes 12595200 | tf_op jit(solution)/shard_map/dot_general | solution.py:594
  80.1 3.6 collective-permute-start.3
  88.8 9.8 %intra.1.yl_ref = f32[1024,1024]{1,0:T(8,128)} custom-call(bf16[1024,1024]{1,0:T(8,128)(2,1)} %get-tuple-element.37.xa_ref, bf16[1024,256]{1,0:T(8,128)(2,1)} %get-tuple-element.38.bca_ref, f32[1024,16]{1,0:T(8,128)} %get-tuple-element.39.dt_ref, f32[1024,16]{1,0:T(8,128)} %get-tuple-element.40.log_ref, bf16[8,128,1024]{2,1,0:T(8,128)(2,1)} %get-tuple-element.41.sloc_ref, ...), custom_call_target="tpu_custom_call" | custom-call | flops 536870912 | bytes 8388608 | tf_op jit(solution)/shard_map/intra/pallas_call | solution.py:621
  102.0 4.6 collective-permute-done.2
  113.8 8.4 %fusion.39.gg_ref = f32[1024,1024]{1,0:T(8,128)} fusion(bf16[1024,2048]{1,0:T(8,128)(2,1)} %constant_dynamic-update-slice_fusion.1, bf16[1024,2048]{1,0:T(8,128)(2,1)S(1)} %copy-done.34), kind=kOutput, calls=%fused_computation.138 | convolution fusion | flops 4294967296 | bytes 12582912 | tf_op jit(solution)/shard_map/dot_general | solution.py:619
  122.2 12.1 %gate_sums.1 = (f32[1024,1024]{1,0:T(8,128)}, bf16[8,128,1024]{2,1,0:T(8,128)(2,1)}, f32[8,8,128]{2,1,0:T(8,128)}) custom-call(f32[1024,1024]{1,0:T(8,128)} %intra.1.yl_ref, bf16[1024,256]{1,0:T(8,128)(2,1)} %get-tuple-element.38.bca_ref, f32[1024,16]{1,0:T(8,128)} %get-tuple-element.40.log_ref, bf16[8,128,1024]{2,1,0:T(8,128)(2,1)} %get-tuple-element.41.sloc_ref, ...), custom_call_target="tpu_custom_call" | custom-call | flops 268435456 | bytes 20971520 | tf_op jit(solution)/shard_map/gate_sums/pallas_call | solution.py:630
  138.5 3.9 collective-permute-done.17
  143.0 13.3 %gate_back.1 = (bf16[1024,1024]{1,0:T(8,128)(2,1)}, bf16[1024,1024]{1,0:T(8,128)(2,1)}, bf16[1024,1024]{1,0:T(8,128)(2,1)}, bf16[8,128,1024]{2,1,0:T(8,128)(2,1)...) custom-call(f32[1024,1024]{1,0:T(8,128)} %get-tuple-element.43.y_ref, ...), custom_call_target="tpu_custom_call" | custom-call | flops 268435456 | bytes 20971520 | tf_op jit(solution)/shard_map/gate_back/pallas_call | solution.py:643
  161.6 20.9 %collective-permute-done.20 = bf16[128,1024]{1,0:T(8,128)(2,1)S(1)} collective-permute-done((bf16[128,1024]{1,0:T(8,128)(2,1)}, bf16[128,1024]{1,0:T(8,128)(2,1)S(1)}, u32[]{:S(2)}, u32[]{:S(2)}) %collective-permute-start.20) | collective-permute-done | bytes 262176 | tf_op jit(solution)/shard_map/ppermute | solution.py:444
  183.4 42.1 %scan_back.1 = (bf16[1024,1024]{1,0:T(8,128)(2,1)}, bf16[1024,256]{1,0:T(8,128)(2,1)}, bf16[1024,16]{1,0:T(8,128)(2,1)}, f32[16,1024]{1,0:T(8,128)}, f32[16,256]...) custom-call(bf16[1024,1024]{1,0:T(8,128)(2,1)} %get-tuple-element.47, ...), custom_call_target="tpu_custom_call" | custom-call | flops 1610612736 | bytes 20971520 | tf_op jit(solution)/shard_map/scan_back/pallas_call | solution.py:682
  240.7 4.5 convolution_convert_fusion.4
  246.4 12.4 %collective-permute-start.61 = (bf16[256,256]{0,1:T(8,128)(2,1)S(1)}, bf16[256,256]{0,1:T(8,128)(2,1)S(1)}, u32[]{:S(2)}, u32[]{:S(2)}) collective-permute-start(bf16[256,256]{0,1:T(8,128)(2,1)S(1)} %constant_dynamic-slice_fusion), channel_id=1, source_target_pairs={{0,8},{8,16},{16,24},{24,28},{28,20},{20,12},{12,4},{4,0},{1,9},{9... | collective-permute-start | bytes 393224 | tf_op jit(solution)/shard_map/ppermute | solution.py:520
  261.4 7.1 %collective-permute-start.62 = (bf16[256,256]{0,1:T(8,128)(2,1)S(1)}, bf16[256,256]{0,1:T(8,128)(2,1)S(1)}, u32[]{:S(2)}, u32[]{:S(2)}) collective-permute-start(bf16[256,256]{0,1:T(8,128)(2,1)S(1)} %add_convert_fusion.38), channel_id=1, source_target_pairs={{0,8},{8,16},{16,24},{24,28},{28,20},{20,12},{12,4},{4,0},{1,9},{9... | collective-permute-start | bytes 393224 | tf_op jit(solution)/shard_map/ppermute | solution.py:520
  295.1 7.9 %convolution_convert_fusion.2 = bf16[2048,1024]{0,1:T(8,128)(2,1)S(1)} fusion(bf16[1024,1024]{1,0:T(8,128)(2,1)} %get-tuple-element.46, bf16[1024,2048]{1,0:T(8,128)(2,1)} %param.18, f32[2048]{0:T(1024)S(1)} %copy-done.27, f32[1024]{0:T(1024)S(1)} %add_rsqrt_fusion), kind=kOutput, calls=%fused_computation.13 | convolution fusion | flops 4305453056 | bytes 10498048 | tf_op jit(solution)/shard_map/dot_general | solution.py:667
  303.5 10.3 %fusion.11 = f32[1024,2048]{1,0:T(8,128)} fusion(bf16[1024,1024]{1,0:T(8,128)(2,1)S(1)} %copy-done.36, bf16[2048,1,1024]{2,1,0:T(2,128)(2,1)} %get-tuple-element.112), kind=kOutput, calls=%fused_computation.29 | convolution fusion | flops 4294967296 | bytes 14680064 | tf_op jit(solution)/shard_map/dot_general | solution.py:720
  323.8 9.5 %convolution_convert_fusion = bf16[2048,1024]{1,0:T(8,128)(2,1)} fusion(bf16[1024,2048]{1,0:T(8,128)(2,1)} %constant_dynamic-update-slice_fusion.1, bf16[1024,1024]{1,0:T(8,128)(2,1)} %get-tuple-element.45), kind=kOutput, calls=%fused_computation.11 | convolution fusion | flops 4297064448 | bytes 10485760 | tf_op jit(solution)/shard_map/dot_general | solution.py:663
  333.3 7.3 %convolution_convert_fusion.3 = bf16[1024,2048]{1,0:T(8,128)(2,1)S(1)} fusion(bf16[1024,1024]{1,0:T(8,128)(2,1)} %get-tuple-element.45, bf16[1024,2048]{1,0:T(8,128)(2,1)} %param.27), kind=kOutput, calls=%fused_computation.14 | convolution fusion | flops 4297064448 | bytes 10485760 | tf_op jit(solution)/shard_map/dot_general | solution.py:671
  359.0 10.4 %fusion.10 = f32[1024,2048]{1,0:T(8,128)} fusion(bf16[1024,1024]{1,0:T(8,128)(2,1)S(1)} %fusion.24, bf16[2048,1,1024]{2,1,0:T(2,128)(2,1)} %get-tuple-element.113), kind=kOutput, calls=%fused_computation.28 | convolution fusion | flops 4294967296 | bytes 14680064 | tf_op jit(solution)/shard_map/dot_general | solution.py:721
  369.5 5.7 convolution_convert_fusion.1
  377.5 8.9 %fusion.4 = (f32[2048]{0:T(1024)S(1)}, f32[1024]{0:T(1024)}, bf16[1024,2048]{1,0:T(8,128)(2,1)S(1)}) fusion(bf16[1024,2048]{1,0:T(8,128)(2,1)S(1)} %copy-done.3, f32[1024]{0:T(1024)S(1)} %add_rsqrt_fusion, f32[2048]{0:T(1024)} %param.19, f32[1024,2048]{1,0:T(8,128)S(1)} %fusion.40, f32[1024,2048]{1,0:T(8,128)} %fusion.11, f32[1024,2048]{1,0:T(8,128)} %fusion.10, ...), kind=kOutput, calls=%fused_computation.8 | convolution fusion | flops 88077312 | bytes 33677312 | tf_op jit(solution)/shard_map/dot_general | solution.py:723
  396.6 4.5 collective-permute-done.30
  406.2 5.5 collective-permute-done.31
  411.7 3.3 collective-permute-start.32
  417.9 3.9 collective-permute-start.54
  442.6 10.7 %collective-permute-done.72 = bf16[256,256]{0,1:T(8,128)(2,1)S(1)} collective-permute-done((bf16[256,256]{0,1:T(8,128)(2,1)S(1)}, bf16[256,256]{0,1:T(8,128)(2,1)S(1)}, u32[]{:S(2)}, u32[]{:S(2)}) %collective-permute-start.72) | collective-permute-done | bytes 131104 | tf_op jit(solution)/shard_map/ppermute | solution.py:520
  457.4 6.3 %collective-permute-done.35 = bf16[256,512]{0,1:T(8,128)(2,1)S(1)} collective-permute-done((bf16[256,512]{0,1:T(8,128)(2,1)S(1)}, bf16[256,512]{0,1:T(8,128)(2,1)S(1)}, u32[]{:S(2)}, u32[]{:S(2)}) %collective-permute-start.35) | collective-permute-done | bytes 262176 | tf_op jit(solution)/shard_map/ppermute | solution.py:520
  463.6 7.2 %collective-permute-start.73 = (bf16[256,256]{0,1:T(8,128)(2,1)S(1)}, bf16[256,256]{0,1:T(8,128)(2,1)S(1)}, u32[]{:S(2)}, u32[]{:S(2)}) collective-permute-start(bf16[256,256]{0,1:T(8,128)(2,1)S(1)} %add_convert_fusion.29), channel_id=1, source_target_pairs={{0,4},{8,0},{16,8},{24,16},{28,24},{20,28},{12,20},{4,12},{1,5},{9... | collective-permute-start | bytes 393224 | tf_op jit(solution)/shard_map/ppermute | solution.py:520
  477.8 3.1 collective-permute-done.48
  487.3 5.2 collective-permute-done.36
  504.1 3.2 collective-permute-done.49
  515.8 3.1 collective-permute-done.37
  524.3 3.5 collective-permute-done.57
  530.7 5.5 collective-permute-done.45
  539.2 6.3 %collective-permute-done.58 = bf16[256,512]{0,1:T(8,128)(2,1)S(1)} collective-permute-done((bf16[256,512]{0,1:T(8,128)(2,1)S(1)}, bf16[256,512]{0,1:T(8,128)(2,1)S(1)}, u32[]{:S(2)}, u32[]{:S(2)}) %collective-permute-start.58) | collective-permute-done | bytes 262176 | tf_op jit(solution)/shard_map/ppermute | solution.py:520
  549.8 3.5 collective-permute-done.46
  553.4 4.1 collective-permute-done.59
  557.5 3.3 collective-permute-done.39
  567.3 6.5 %collective-permute-done.53 = bf16[256,512]{0,1:T(8,128)(2,1)S(1)} collective-permute-done((bf16[256,512]{0,1:T(8,128)(2,1)S(1)}, bf16[256,512]{0,1:T(8,128)(2,1)S(1)}, u32[]{:S(2)}, u32[]{:S(2)}) %collective-permute-start.53) | collective-permute-done | bytes 262176 | tf_op jit(solution)/shard_map/ppermute | solution.py:520
  576.5 4.4 collective-permute-done.25
  580.9 5.3 fusion.9
  (351 shorter events, 198.4 us)
Async XLA Ops:
  7.2 579.0 %all-gather.2.cloned.1.call-start = ((), (), s32[]{:S(2)}) async-start(), calls=%async_computation.1 | async-start | bytes 1179648 | tf_op jit(solution)/shard_map/all_gather | solution.py:755
  7.3 93.3 %collective-permute-start.6 = (bf16[1024,512]{1,0:T(8,128)(2,1)}, bf16[1024,512]{1,0:T(8,128)(2,1)}, u32[]{:S(2)}, u32[]{:S(2)}) collective-permute-start(bf16[1024,512]{1,0:T(8,128)(2,1)} %param.29), channel_id=1, source_target_pairs={{0,2},{1,3},{2,0},{3,1},{4,6},{5,7},{6,4},{7,5},{8,10},{9,11},{10,... | collective-permute-start | bytes 3145736 | tf_op jit(solution)/shard_map/ppermute | solution.py:448
  10.3 100.1 %collective-permute-start.7 = (bf16[1024,512]{1,0:T(8,128)(2,1)}, bf16[1024,512]{1,0:T(8,128)(2,1)}, u32[]{:S(2)}, u32[]{:S(2)}) collective-permute-start(bf16[1024,512]{1,0:T(8,128)(2,1)} %param.29), channel_id=1, source_target_pairs={{0,1},{1,0},{2,3},{3,2},{4,5},{5,4},{6,7},{7,6},{8,9},{9,8},{10,11... | collective-permute-start | bytes 3145736 | tf_op jit(solution)/shard_map/ppermute | solution.py:448
  15.7 35.5 %collective-permute-start.1 = (bf16[16,256]{1,0:T(8,128)(2,1)S(1)}, bf16[16,256]{1,0:T(8,128)(2,1)S(1)}, u32[]{:S(2)}, u32[]{:S(2)}) collective-permute-start(bf16[16,256]{1,0:T(8,128)(2,1)S(1)} %slice.210), channel_id=1, source_target_pairs={{0,4},{4,8},{8,12},{12,16},{16,20},{20,24},{24,28},{1,5},{5,9},{9,... | collective-permute-start | bytes 24584 | tf_op jit(solution)/shard_map/ppermute | solution.py:444
  41.2 10.0 %collective-permute-start = (bf16[16,1024]{1,0:T(8,128)(2,1)S(1)}, bf16[16,1024]{1,0:T(8,128)(2,1)S(1)}, u32[]{:S(2)}, u32[]{:S(2)}) collective-permute-start(bf16[16,1024]{1,0:T(8,128)(2,1)S(1)} %slice.209), channel_id=1, source_target_pairs={{0,4},{4,8},{8,12},{12,16},{16,20},{20,24},{24,28},{1,5},{5,9},{9,... | collective-permute-start | bytes 98312 | tf_op jit(solution)/shard_map/ppermute | solution.py:444
  65.3 33.2 %collective-permute-start.4 = (bf16[144,1024]{1,0:T(8,128)(2,1)}, bf16[144,1024]{1,0:T(8,128)(2,1)S(1)}, u32[]{:S(2)}, u32[]{:S(2)}) collective-permute-start(bf16[144,1024]{1,0:T(8,128)(2,1)} %get-tuple-element.42), channel_id=1, source_target_pairs={{0,12},{4,16},{8,20},{12,24},{16,28},{1,13},{5,17},{9,21},{13,25},... | collective-permute-start | bytes 884744 | tf_op jit(solution)/shard_map/ppermute | solution.py:444
  80.1 20.6 %collective-permute-start.3 = (bf16[144,1024]{1,0:T(8,128)(2,1)S(1)}, bf16[144,1024]{1,0:T(8,128)(2,1)S(1)}, u32[]{:S(2)}, u32[]{:S(2)}) collective-permute-start(bf16[144,1024]{1,0:T(8,128)(2,1)S(1)} %copy-done.33), channel_id=1, source_target_pairs={{0,8},{4,12},{8,16},{12,20},{16,24},{20,28},{1,9},{5,13},{9,17},{1... | collective-permute-start | bytes 884744 | tf_op jit(solution)/shard_map/ppermute | solution.py:444
  87.3 19.4 %collective-permute-start.5 = (bf16[144,1024]{1,0:T(8,128)(2,1)S(1)}, bf16[144,1024]{1,0:T(8,128)(2,1)S(1)}, u32[]{:S(2)}, u32[]{:S(2)}) collective-permute-start(bf16[144,1024]{1,0:T(8,128)(2,1)S(1)} %copy-done.33), channel_id=1, source_target_pairs={{0,16},{4,20},{8,24},{12,28},{1,17},{5,21},{9,25},{13,29},{2,18},{... | collective-permute-start | bytes 884744 | tf_op jit(solution)/shard_map/ppermute | solution.py:444
  100.6 12.2 %collective-permute-start.8 = (bf16[1024,512]{1,0:T(8,128)(2,1)}, bf16[1024,512]{1,0:T(8,128)(2,1)S(1)}, u32[]{:S(2)}, u32[]{:S(2)}) collective-permute-start(bf16[1024,512]{1,0:T(8,128)(2,1)} %collective-permute-done.6), channel_id=1, source_target_pairs={{0,1},{1,0},{2,3},{3,2},{4,5},{5,4},{6,7},{7,6},{8,9},{9,8},{10,11... | collective-permute-start | bytes 3145736 | tf_op jit(solution)/shard_map/ppermute | solution.py:448
  100.7 36.3 %collective-permute-start.19 = (bf16[16,1024]{1,0:T(8,128)(2,1)S(1)}, bf16[16,1024]{1,0:T(8,128)(2,1)S(1)}, u32[]{:S(2)}, u32[]{:S(2)}) collective-permute-start(bf16[16,1024]{1,0:T(8,128)(2,1)S(1)} %slice.183), channel_id=1, source_target_pairs={{12,0},{16,4},{20,8},{24,12},{28,16},{13,1},{17,5},{21,9},{25,13},... | collective-permute-start | bytes 98312 | tf_op jit(solution)/shard_map/ppermute | solution.py:444
  135.7 25.9 %collective-permute-start.15 = (bf16[16,1024]{1,0:T(8,128)(2,1)S(1)}, bf16[16,1024]{1,0:T(8,128)(2,1)S(1)}, u32[]{:S(2)}, u32[]{:S(2)}) collective-permute-start(bf16[16,1024]{1,0:T(8,128)(2,1)S(1)} %slice.183), channel_id=1, source_target_pairs={{4,0},{8,4},{12,8},{16,12},{20,16},{24,20},{28,24},{5,1},{9,5},{13... | collective-permute-start | bytes 98312 | tf_op jit(solution)/shard_map/ppermute | solution.py:444
  156.3 26.1 %collective-permute-start.20 = (bf16[128,1024]{1,0:T(8,128)(2,1)}, bf16[128,1024]{1,0:T(8,128)(2,1)S(1)}, u32[]{:S(2)}, u32[]{:S(2)}) collective-permute-start(bf16[128,1024]{1,0:T(8,128)(2,1)} %get-tuple-element.50), channel_id=1, source_target_pairs={{16,0},{20,4},{24,8},{28,12},{17,1},{21,5},{25,9},{29,13},{18,2},{... | collective-permute-start | bytes 786440 | tf_op jit(solution)/shard_map/ppermute | solution.py:444
  157.6 24.8 %collective-permute-start.18 = (bf16[128,1024]{1,0:T(8,128)(2,1)}, bf16[128,1024]{1,0:T(8,128)(2,1)S(1)}, u32[]{:S(2)}, u32[]{:S(2)}) collective-permute-start(bf16[128,1024]{1,0:T(8,128)(2,1)} %get-tuple-element.50), channel_id=1, source_target_pairs={{12,0},{16,4},{20,8},{24,12},{28,16},{13,1},{17,5},{21,9},{25,13},... | collective-permute-start | bytes 786440 | tf_op jit(solution)/shard_map/ppermute | solution.py:444
  158.9 23.5 %collective-permute-start.16 = (bf16[128,1024]{1,0:T(8,128)(2,1)}, bf16[128,1024]{1,0:T(8,128)(2,1)S(1)}, u32[]{:S(2)}, u32[]{:S(2)}) collective-permute-start(bf16[128,1024]{1,0:T(8,128)(2,1)} %get-tuple-element.50), channel_id=1, source_target_pairs={{8,0},{12,4},{16,8},{20,12},{24,16},{28,20},{9,1},{13,5},{17,9},{2... | collective-permute-start | bytes 786440 | tf_op jit(solution)/shard_map/ppermute | solution.py:444
  160.2 22.2 %collective-permute-start.14 = (bf16[128,1024]{1,0:T(8,128)(2,1)}, bf16[128,1024]{1,0:T(8,128)(2,1)S(1)}, u32[]{:S(2)}, u32[]{:S(2)}) collective-permute-start(bf16[128,1024]{1,0:T(8,128)(2,1)} %get-tuple-element.50), channel_id=1, source_target_pairs={{4,0},{8,4},{12,8},{16,12},{20,16},{24,20},{28,24},{5,1},{9,5},{13... | collective-permute-start | bytes 786440 | tf_op jit(solution)/shard_map/ppermute | solution.py:444
  225.5 13.8 %collective-permute-start.22 = (f32[16,256]{1,0:T(8,128)}, f32[16,256]{1,0:T(8,128)S(1)}, u32[]{:S(2)}, u32[]{:S(2)}) collective-permute-start(f32[16,256]{1,0:T(8,128)} %get-tuple-element.56), channel_id=1, source_target_pairs={{4,0},{8,4},{12,8},{16,12},{20,16},{24,20},{28,24},{5,1},{9,5},{13... | collective-permute-start | bytes 49160 | tf_op jit(solution)/shard_map/ppermute | solution.py:444
  246.4 14.9 %collective-permute-start.61 = (bf16[256,256]{0,1:T(8,128)(2,1)S(1)}, bf16[256,256]{0,1:T(8,128)(2,1)S(1)}, u32[]{:S(2)}, u32[]{:S(2)}) collective-permute-start(bf16[256,256]{0,1:T(8,128)(2,1)S(1)} %constant_dynamic-slice_fusion), channel_id=1, source_target_pairs={{0,8},{8,16},{16,24},{24,28},{28,20},{20,12},{12,4},{4,0},{1,9},{9... | collective-permute-start | bytes 393224 | tf_op jit(solution)/shard_map/ppermute | solution.py:520
  261.4 10.5 %collective-permute-start.62 = (bf16[256,256]{0,1:T(8,128)(2,1)S(1)}, bf16[256,256]{0,1:T(8,128)(2,1)S(1)}, u32[]{:S(2)}, u32[]{:S(2)}) collective-permute-start(bf16[256,256]{0,1:T(8,128)(2,1)S(1)} %add_convert_fusion.38), channel_id=1, source_target_pairs={{0,8},{8,16},{16,24},{24,28},{28,20},{20,12},{12,4},{4,0},{1,9},{9... | collective-permute-start | bytes 393224 | tf_op jit(solution)/shard_map/ppermute | solution.py:520
  283.3 9.3 %collective-permute-start.65 = (bf16[256,256]{0,1:T(8,128)(2,1)S(1)}, bf16[256,256]{0,1:T(8,128)(2,1)S(1)}, u32[]{:S(2)}, u32[]{:S(2)}) collective-permute-start(bf16[256,256]{0,1:T(8,128)(2,1)S(1)} %add_convert_fusion.35), channel_id=1, source_target_pairs={{0,8},{8,16},{16,24},{24,28},{28,20},{20,12},{12,4},{4,0},{1,9},{9... | collective-permute-start | bytes 393224 | tf_op jit(solution)/shard_map/ppermute | solution.py:520
  292.7 10.3 %collective-permute-start.66 = (bf16[256,256]{0,1:T(8,128)(2,1)S(1)}, bf16[256,256]{0,1:T(8,128)(2,1)S(1)}, u32[]{:S(2)}, u32[]{:S(2)}) collective-permute-start(bf16[256,256]{0,1:T(8,128)(2,1)S(1)} %add_convert_fusion.34), channel_id=1, source_target_pairs={{0,8},{8,16},{16,24},{24,28},{28,20},{20,12},{12,4},{4,0},{1,9},{9... | collective-permute-start | bytes 393224 | tf_op jit(solution)/shard_map/ppermute | solution.py:520
  303.1 10.6 %collective-permute-start.67 = (bf16[256,256]{0,1:T(8,128)(2,1)S(1)}, bf16[256,256]{0,1:T(8,128)(2,1)S(1)}, u32[]{:S(2)}, u32[]{:S(2)}) collective-permute-start(bf16[256,256]{0,1:T(8,128)(2,1)S(1)} %add_convert_fusion.33), channel_id=1, source_target_pairs={{0,8},{8,16},{16,24},{24,28},{28,20},{20,12},{12,4},{4,0},{1,9},{9... | collective-permute-start | bytes 393224 | tf_op jit(solution)/shard_map/ppermute | solution.py:520
  319.0 28.6 %collective-permute-start.40 = (bf16[256,512]{0,1:T(8,128)(2,1)}, bf16[256,512]{0,1:T(8,128)(2,1)}, u32[]{:S(2)}, u32[]{:S(2)}) collective-permute-start(bf16[256,512]{0,1:T(8,128)(2,1)} %constant_dynamic-slice_fusion.5), channel_id=1, source_target_pairs={{0,4},{8,0},{16,8},{24,16},{28,24},{20,28},{12,20},{4,12},{1,5},{9... | collective-permute-start | bytes 786440 | tf_op jit(solution)/shard_map/ppermute | solution.py:520
  321.4 31.3 %collective-permute-start.33 = (bf16[256,512]{0,1:T(8,128)(2,1)}, bf16[256,512]{0,1:T(8,128)(2,1)}, u32[]{:S(2)}, u32[]{:S(2)}) collective-permute-start(bf16[256,512]{0,1:T(8,128)(2,1)} %constant_dynamic-slice_fusion.6), channel_id=1, source_target_pairs={{0,8},{8,16},{16,24},{24,28},{28,20},{20,12},{12,4},{4,0},{1,9},{9... | collective-permute-start | bytes 786440 | tf_op jit(solution)/shard_map/ppermute | solution.py:520
  323.8 265.0 %reduce-scatter.2.cloned.1.call-start = ((), (), s32[]{:S(2)}) async-start(), calls=%async_computation.2 | async-start | bytes 4718592 | tf_op jit(solution)/shard_map/reduce_scatter | solution.py:666
  344.2 232.2 %collective-permute-start.11 = (bf16[1024,512]{1,0:T(8,128)(2,1)}, bf16[1024,512]{1,0:T(8,128)(2,1)}, u32[]{:S(2)}, u32[]{:S(2)}) collective-permute-start(bf16[1024,512]{1,0:T(8,128)(2,1)} %get-tuple-element.122), channel_id=1, source_target_pairs={{0,1},{1,0},{2,3},{3,2},{4,5},{5,4},{6,7},{7,6},{8,9},{9,8},{10,11... | collective-permute-start | bytes 3145736 | tf_op jit(solution)/shard_map/ppermute | solution.py:448
  344.2 150.4 %collective-permute-start.12 = (bf16[1024,512]{1,0:T(8,128)(2,1)}, bf16[1024,512]{1,0:T(8,128)(2,1)}, u32[]{:S(2)}, u32[]{:S(2)}) collective-permute-start(bf16[1024,512]{1,0:T(8,128)(2,1)} %get-tuple-element.123), channel_id=1, source_target_pairs={{0,1},{1,0},{2,3},{3,2},{4,5},{5,4},{6,7},{7,6},{8,9},{9,8},{10,11... | collective-permute-start | bytes 3145736 | tf_op jit(solution)/shard_map/ppermute | solution.py:448
  346.3 12.7 %collective-permute-start.21 = (f32[16,1024]{1,0:T(8,128)S(1)}, f32[16,1024]{1,0:T(8,128)S(1)}, u32[]{:S(2)}, u32[]{:S(2)}) collective-permute-start(f32[16,1024]{1,0:T(8,128)S(1)} %copy-done.37), channel_id=1, source_target_pairs={{4,0},{8,4},{12,8},{16,12},{20,16},{24,20},{28,24},{5,1},{9,5},{13... | collective-permute-start | bytes 196616 | tf_op jit(solution)/shard_map/ppermute | solution.py:444
  349.4 81.1 %collective-permute-start.41 = (bf16[256,512]{0,1:T(8,128)(2,1)}, bf16[256,512]{0,1:T(8,128)(2,1)}, u32[]{:S(2)}, u32[]{:S(2)}) collective-permute-start(bf16[256,512]{0,1:T(8,128)(2,1)} %add_convert_fusion.19), channel_id=1, source_target_pairs={{0,4},{8,0},{16,8},{24,16},{28,24},{20,28},{12,20},{4,12},{1,5},{9... | collective-permute-start | bytes 786440 | tf_op jit(solution)/shard_map/ppermute | solution.py:520
  358.5 53.2 %collective-permute-start.70 = (bf16[256,256]{0,1:T(8,128)(2,1)}, bf16[256,256]{0,1:T(8,128)(2,1)}, u32[]{:S(2)}, u32[]{:S(2)}) collective-permute-start(bf16[256,256]{0,1:T(8,128)(2,1)} %constant_dynamic-slice_fusion.1), channel_id=1, source_target_pairs={{0,4},{8,0},{16,8},{24,16},{28,24},{20,28},{12,20},{4,12},{1,5},{9... | collective-permute-start | bytes 393224 | tf_op jit(solution)/shard_map/ppermute | solution.py:520
  411.7 17.5 %collective-permute-start.34 = (bf16[256,512]{0,1:T(8,128)(2,1)}, bf16[256,512]{0,1:T(8,128)(2,1)}, u32[]{:S(2)}, u32[]{:S(2)}) collective-permute-start(bf16[256,512]{0,1:T(8,128)(2,1)} %add_convert_fusion.25), channel_id=1, source_target_pairs={{0,8},{8,16},{16,24},{24,28},{28,20},{20,12},{12,4},{4,0},{1,9},{9... | collective-permute-start | bytes 786440 | tf_op jit(solution)/shard_map/ppermute | solution.py:520
  417.9 18.6 %collective-permute-start.54 = (bf16[256,512]{0,1:T(8,128)(2,1)}, bf16[256,512]{0,1:T(8,128)(2,1)}, u32[]{:S(2)}, u32[]{:S(2)}) collective-permute-start(bf16[256,512]{0,1:T(8,128)(2,1)} %constant_dynamic-slice_fusion.3), channel_id=1, source_target_pairs={{0,4},{8,0},{16,8},{24,16},{28,24},{20,28},{12,20},{4,12},{1,5},{9... | collective-permute-start | bytes 786440 | tf_op jit(solution)/shard_map/ppermute | solution.py:520
  429.2 10.9 %collective-permute-start.47 = (bf16[256,512]{0,1:T(8,128)(2,1)S(1)}, bf16[256,512]{0,1:T(8,128)(2,1)S(1)}, u32[]{:S(2)}, u32[]{:S(2)}) collective-permute-start(bf16[256,512]{0,1:T(8,128)(2,1)S(1)} %constant_dynamic-slice_fusion.2), channel_id=1, source_target_pairs={{0,8},{8,16},{16,24},{24,28},{28,20},{20,12},{12,4},{4,0},{1,9},{9... | collective-permute-start | bytes 786440 | tf_op jit(solution)/shard_map/ppermute | solution.py:520
  435.5 140.9 %collective-permute-start.23 = (bf16[1024,512]{1,0:T(8,128)(2,1)}, bf16[1024,512]{1,0:T(8,128)(2,1)}, u32[]{:S(2)}, u32[]{:S(2)}) collective-permute-start(bf16[1024,512]{1,0:T(8,128)(2,1)} %get-tuple-element.120), channel_id=1, source_target_pairs={{0,1},{1,0},{2,3},{3,2},{4,5},{5,4},{6,7},{7,6},{8,9},{9,8},{10,11... | collective-permute-start | bytes 3145736 | tf_op jit(solution)/shard_map/ppermute | solution.py:448
  436.5 17.8 %collective-permute-start.42 = (bf16[256,512]{0,1:T(8,128)(2,1)S(1)}, bf16[256,512]{0,1:T(8,128)(2,1)S(1)}, u32[]{:S(2)}, u32[]{:S(2)}) collective-permute-start(bf16[256,512]{0,1:T(8,128)(2,1)S(1)} %add_convert_fusion.18), channel_id=1, source_target_pairs={{0,4},{8,0},{16,8},{24,16},{28,24},{20,28},{12,20},{4,12},{1,5},{9... | collective-permute-start | bytes 786440 | tf_op jit(solution)/shard_map/ppermute | solution.py:520
  440.1 13.2 %collective-permute-start.72 = (bf16[256,256]{0,1:T(8,128)(2,1)S(1)}, bf16[256,256]{0,1:T(8,128)(2,1)S(1)}, u32[]{:S(2)}, u32[]{:S(2)}) collective-permute-start(bf16[256,256]{0,1:T(8,128)(2,1)S(1)} %add_convert_fusion.30), channel_id=1, source_target_pairs={{0,4},{8,0},{16,8},{24,16},{28,24},{20,28},{12,20},{4,12},{1,5},{9... | collective-permute-start | bytes 393224 | tf_op jit(solution)/shard_map/ppermute | solution.py:520
  453.3 10.3 %collective-permute-start.35 = (bf16[256,512]{0,1:T(8,128)(2,1)S(1)}, bf16[256,512]{0,1:T(8,128)(2,1)S(1)}, u32[]{:S(2)}, u32[]{:S(2)}) collective-permute-start(bf16[256,512]{0,1:T(8,128)(2,1)S(1)} %add_convert_fusion.24), channel_id=1, source_target_pairs={{0,8},{8,16},{16,24},{24,28},{28,20},{20,12},{12,4},{4,0},{1,9},{9... | collective-permute-start | bytes 786440 | tf_op jit(solution)/shard_map/ppermute | solution.py:520
  454.3 20.2 %collective-permute-start.55 = (bf16[256,512]{0,1:T(8,128)(2,1)S(1)}, bf16[256,512]{0,1:T(8,128)(2,1)S(1)}, u32[]{:S(2)}, u32[]{:S(2)}) collective-permute-start(bf16[256,512]{0,1:T(8,128)(2,1)S(1)} %add_convert_fusion.7), channel_id=1, source_target_pairs={{0,4},{8,0},{16,8},{24,16},{28,24},{20,28},{12,20},{4,12},{1,5},{9... | collective-permute-start | bytes 786440 | tf_op jit(solution)/shard_map/ppermute | solution.py:520
  463.6 9.7 %collective-permute-start.73 = (bf16[256,256]{0,1:T(8,128)(2,1)S(1)}, bf16[256,256]{0,1:T(8,128)(2,1)S(1)}, u32[]{:S(2)}, u32[]{:S(2)}) collective-permute-start(bf16[256,256]{0,1:T(8,128)(2,1)S(1)} %add_convert_fusion.29), channel_id=1, source_target_pairs={{0,4},{8,0},{16,8},{24,16},{28,24},{20,28},{12,20},{4,12},{1,5},{9... | collective-permute-start | bytes 393224 | tf_op jit(solution)/shard_map/ppermute | solution.py:520
  474.5 12.6 %collective-permute-start.43 = (bf16[256,512]{0,1:T(8,128)(2,1)S(1)}, bf16[256,512]{0,1:T(8,128)(2,1)S(1)}, u32[]{:S(2)}, u32[]{:S(2)}) collective-permute-start(bf16[256,512]{0,1:T(8,128)(2,1)S(1)} %add_convert_fusion.17), channel_id=1, source_target_pairs={{0,4},{8,0},{16,8},{24,16},{28,24},{20,28},{12,20},{4,12},{1,5},{9... | collective-permute-start | bytes 786440 | tf_op jit(solution)/shard_map/ppermute | solution.py:520
  487.1 34.1 %collective-permute-start.24 = (bf16[1024,512]{1,0:T(8,128)(2,1)S(1)}, bf16[1024,512]{1,0:T(8,128)(2,1)S(1)}, u32[]{:S(2)}, u32[]{:S(2)}) collective-permute-start(bf16[1024,512]{1,0:T(8,128)(2,1)S(1)} %copy-done.17), channel_id=1, source_target_pairs={{0,1},{1,0},{2,3},{3,2},{4,5},{5,4},{6,7},{7,6},{8,9},{9,8},{10,11... | collective-permute-start | bytes 3145736 | tf_op jit(solution)/shard_map/ppermute | solution.py:448
  492.5 9.4 %collective-permute-start.56 = (bf16[256,512]{0,1:T(8,128)(2,1)S(1)}, bf16[256,512]{0,1:T(8,128)(2,1)S(1)}, u32[]{:S(2)}, u32[]{:S(2)}) collective-permute-start(bf16[256,512]{0,1:T(8,128)(2,1)S(1)} %add_convert_fusion.6), channel_id=1, source_target_pairs={{0,4},{8,0},{16,8},{24,16},{28,24},{20,28},{12,20},{4,12},{1,5},{9... | collective-permute-start | bytes 786440 | tf_op jit(solution)/shard_map/ppermute | solution.py:520
  501.9 12.4 %collective-permute-start.44 = (bf16[256,512]{0,1:T(8,128)(2,1)S(1)}, bf16[256,512]{0,1:T(8,128)(2,1)S(1)}, u32[]{:S(2)}, u32[]{:S(2)}) collective-permute-start(bf16[256,512]{0,1:T(8,128)(2,1)S(1)} %add_convert_fusion.16), channel_id=1, source_target_pairs={{0,4},{8,0},{16,8},{24,16},{28,24},{20,28},{12,20},{4,12},{1,5},{9... | collective-permute-start | bytes 786440 | tf_op jit(solution)/shard_map/ppermute | solution.py:520
  514.3 62.1 %collective-permute-start.13 = (bf16[1024,512]{1,0:T(8,128)(2,1)}, bf16[1024,512]{1,0:T(8,128)(2,1)}, u32[]{:S(2)}, u32[]{:S(2)}) collective-permute-start(bf16[1024,512]{1,0:T(8,128)(2,1)} %add_convert_fusion.1), channel_id=1, source_target_pairs={{0,2},{1,3},{2,0},{3,1},{4,6},{5,7},{6,4},{7,5},{8,10},{9,11},{10,... | collective-permute-start | bytes 3145736 | tf_op jit(solution)/shard_map/ppermute | solution.py:448
  521.2 9.2 %collective-permute-start.50 = (bf16[256,512]{0,1:T(8,128)(2,1)S(1)}, bf16[256,512]{0,1:T(8,128)(2,1)S(1)}, u32[]{:S(2)}, u32[]{:S(2)}) collective-permute-start(bf16[256,512]{0,1:T(8,128)(2,1)S(1)} %add_convert_fusion.11), channel_id=1, source_target_pairs={{0,8},{8,16},{16,24},{24,28},{28,20},{20,12},{12,4},{4,0},{1,9},{9... | collective-permute-start | bytes 786440 | tf_op jit(solution)/shard_map/ppermute | solution.py:520
  536.2 9.2 %collective-permute-start.58 = (bf16[256,512]{0,1:T(8,128)(2,1)S(1)}, bf16[256,512]{0,1:T(8,128)(2,1)S(1)}, u32[]{:S(2)}, u32[]{:S(2)}) collective-permute-start(bf16[256,512]{0,1:T(8,128)(2,1)S(1)} %add_convert_fusion.4), channel_id=1, source_target_pairs={{0,4},{8,0},{16,8},{24,16},{28,24},{20,28},{12,20},{4,12},{1,5},{9... | collective-permute-start | bytes 786440 | tf_op jit(solution)/shard_map/ppermute | solution.py:520
  538.8 9.2 %collective-permute-start.51 = (bf16[256,512]{0,1:T(8,128)(2,1)S(1)}, bf16[256,512]{0,1:T(8,128)(2,1)S(1)}, u32[]{:S(2)}, u32[]{:S(2)}) collective-permute-start(bf16[256,512]{0,1:T(8,128)(2,1)S(1)} %add_convert_fusion.10), channel_id=1, source_target_pairs={{0,8},{8,16},{16,24},{24,28},{28,20},{20,12},{12,4},{4,0},{1,9},{9... | collective-permute-start | bytes 786440 | tf_op jit(solution)/shard_map/ppermute | solution.py:520
  548.0 9.4 %collective-permute-start.59 = (bf16[256,512]{0,1:T(8,128)(2,1)S(1)}, bf16[256,512]{0,1:T(8,128)(2,1)S(1)}, u32[]{:S(2)}, u32[]{:S(2)}) collective-permute-start(bf16[256,512]{0,1:T(8,128)(2,1)S(1)} %add_convert_fusion.3), channel_id=1, source_target_pairs={{0,4},{8,0},{16,8},{24,16},{28,24},{20,28},{12,20},{4,12},{1,5},{9... | collective-permute-start | bytes 786440 | tf_op jit(solution)/shard_map/ppermute | solution.py:520
  565.7 15.1 %collective-permute-start.25 = (bf16[1024,512]{1,0:T(8,128)(2,1)}, bf16[1024,512]{1,0:T(8,128)(2,1)}, u32[]{:S(2)}, u32[]{:S(2)}) collective-permute-start(bf16[1024,512]{1,0:T(8,128)(2,1)} %add_convert_fusion), channel_id=1, source_target_pairs={{0,2},{1,3},{2,0},{3,1},{4,6},{5,7},{6,4},{7,5},{8,10},{9,11},{10,... | collective-permute-start | bytes 3145736 | tf_op jit(solution)/shard_map/ppermute | solution.py:448
  (73 other events, 866.7 us)
Sparse Core Ops, SparseCore 0:
  323.9 43.5 all-gather.1
  371.1 99.7 reduce-scatter.1
